TPU v7x, 512 devices: a whole 4x4x16 slice. The times are simulated.
512 devices in a mesh: gz: 64 (over z, y_hi, core), xy: 8 (over y_lo, x).
Axes of the slice: x: 4, y: 4 (y_hi: 2, y_lo: 2; y = y_hi * 2 + y_lo), z: 16, core: 2. Of those that a mesh axis runs over, the one named last changes fastest.
Arguments:
- patch_features: bfloat16 [16, 640, 144, 128], P(None, 'gz', 'xy'), may hold values from -6 to 6
- conv1_weight: bfloat16 [16, 16, 3, 3, 3], replicated, may hold values from -0.3125 to 0.3125
- conv1_bias: float32 [16], replicated, may hold values from -3 to 3
- conv2_weight: bfloat16 [16, 16, 3, 3, 3], replicated, may hold values from -0.3125 to 0.3125
- conv2_bias: float32 [16], replicated, may hold values from -3 to 3
- head_weight: bfloat16 [16], replicated, may hold values from -3 to 3
- tissue_mask: int32 [512, 128, 128], P('gz', 'xy'), may hold values 0 or 1
Outputs:
- probability: float32 [512, 128, 128], P('gz', 'xy')
- vesselness: float32 [512, 128, 128], P('gz', 'xy')
All inputs are finite; a program needn't handle non-finite values. No bound on the sum of `tissue_mask` on one device may be relied on, other than what follows from the above.
Results may differ from a plain program's by a relative error of at most 0.0025.
The roundings to bfloat16 on the way count: a program that leaves them out, or rounds other values in their place, can miss the bound.
Values sent between devices are 32-bit elements; how exact they have to be, the bound alone decides.
No kernel may reach another device: no remote copies, remote signals or barrier semaphores. Data moves between devices by JAX's collectives and lax.ppermute only.
A program may use at most 128 MiB of HBM per device.

v0:
```python
import jax
import jax.numpy as jnp
from jax import lax
from jax.sharding import PartitionSpec as P

RIM = 8


CONV_DIMS = ("NCDHW", "OIDHW", "NCDHW")
VESSEL_GAIN = 4.0
TUBE_FLOOR = 0.01


def from_behind(block, axis, distance):
    devices = range(lax.axis_size(axis))
    route = [(i - distance, i) for i in devices if i - distance in devices]
    return lax.ppermute(block, axis, route)


def with_halo(x, sides, width):
    for axis, dim in sides:
        count, length = (lax.axis_size(axis), x.shape[dim])
        up = [(i, (i + 1) % count) for i in range(count - 1)]
        down = [(j, i) for i, j in up]
        last = lax.slice_in_dim(x, length - width, length, axis=dim)
        initial = lax.slice_in_dim(x, 0, width, axis=dim)
        before = lax.ppermute(last, axis, up)
        after = lax.ppermute(initial, axis, down)
        x = jnp.concatenate([before, x, after], axis=dim)
    return x


def window(size):
    position = jnp.arange(size).astype(jnp.float32)
    return jnp.exp(-0.5 * ((position - (size - 1) / 2.0) / (size / 4.0)) ** 2)


def conv_layer(inputs, weight, bias):
    summed = lax.conv_general_dilated(
        inputs[None],
        weight,
        (1, 1, 1),
        "SAME",
        dimension_numbers=CONV_DIMS,
        preferred_element_type=jnp.float32,
    )[0]
    return jax.nn.relu(summed + bias[:, None, None, None]).astype(jnp.bfloat16)


def coverage(core, margin, position_idx, axis_count):
    weights = window(core + 2 * margin)
    own_part = weights[margin : margin + core]
    lower_part = jnp.pad(weights[core + margin :], (0, core - margin)) * (position_idx > 0).astype(
        jnp.float32
    )
    upper_part = jnp.pad(weights[:margin], (core - margin, 0)) * (
        position_idx < axis_count - 1
    ).astype(jnp.float32)
    return own_part + lower_part + upper_part


def place_at(piece, z_widths, x_widths):
    return jnp.pad(piece, (z_widths, x_widths, (0, 0)))


def band_matrix(out_len, in_len, offset, radius, degree):
    distance = (jnp.arange(out_len)[:, None] + offset - jnp.arange(in_len)[None, :]).astype(
        jnp.float32
    )
    spread = radius / 3.0
    offsets = jnp.arange(-radius, radius + 1).astype(jnp.float32)
    bell_sum = jnp.sum(jnp.exp(-offsets * offsets / (2.0 * spread * spread)))
    gaussian = (
        jnp.where(
            jnp.abs(distance) <= radius,
            jnp.exp(-distance * distance / (2.0 * spread * spread)),
            0.0,
        )
        / bell_sum
    )
    if degree == 1:
        return -distance / (spread * spread) * gaussian
    if degree == 2:
        return (distance * distance / spread**4 - 1.0 / (spread * spread)) * gaussian
    return gaussian


def tubeness(hzz, hxx, hyy, hzx, hzy, hxy):
    first_inv = hzz + hxx + hyy
    second_inv = hzz * hxx + hzz * hyy + hxx * hyy - hzx * hzx - hzy * hzy - hxy * hxy
    third_inv = (
        hzz * (hxx * hyy - hxy * hxy)
        - hzx * (hzx * hyy - hxy * hzy)
        + hzy * (hzx * hxy - hxx * hzy)
    )
    positive = jax.nn.relu(second_inv)
    return (
        jax.nn.relu(-first_inv)
        * positive
        / (positive + jnp.cbrt(third_inv * third_inv) + TUBE_FLOOR)
    )


def hessian_tube(extended, core_z, core_x, y_cells, radius):
    highest = lax.Precision.HIGHEST
    scale_sq = (radius / 3.0) ** 2

    def pass_z(degree):
        return jnp.einsum(
            "ij,jxy->ixy",
            band_matrix(core_z, core_z + 2 * RIM, RIM, radius, degree),
            extended,
            precision=highest,
        )

    def pass_x(volume, degree):
        return jnp.einsum(
            "ij,zjy->ziy",
            band_matrix(core_x, core_x + 2 * RIM, RIM, radius, degree),
            volume,
            precision=highest,
        )

    def pass_y(volume, degree):
        return jnp.einsum(
            "zxj,ij->zxi",
            volume,
            band_matrix(y_cells, y_cells, 0, radius, degree),
            precision=highest,
        )

    along_z = [pass_z(degree) for degree in range(3)]
    flat_flat = pass_x(along_z[0], 0)
    flat_slope = pass_x(along_z[0], 1)
    flat_curve = pass_x(along_z[0], 2)
    slope_flat = pass_x(along_z[1], 0)
    slope_slope = pass_x(along_z[1], 1)
    curve_flat = pass_x(along_z[2], 0)
    hzz = scale_sq * pass_y(curve_flat, 0)
    hxx = scale_sq * pass_y(flat_curve, 0)
    hyy = scale_sq * pass_y(flat_flat, 2)
    hzx = scale_sq * pass_y(slope_slope, 0)
    hzy = scale_sq * pass_y(slope_flat, 1)
    hxy = scale_sq * pass_y(flat_slope, 1)
    return tubeness(hzz, hxx, hyy, hzx, hzy, hxy)


def on_device(
    patch_features, conv1_weight, conv1_bias, conv2_weight, conv2_bias, head_weight, tissue_mask
):
    core_z, core_x, y_cells = tissue_mask.shape
    span_z = patch_features.shape[1]
    span_x = patch_features.shape[2]
    margin = (span_z - core_z) // 2
    hidden = conv_layer(patch_features, conv1_weight, conv1_bias)
    hidden = conv_layer(hidden, conv2_weight, conv2_bias)
    logits = jnp.einsum("c,czxy->zxy", head_weight, hidden, preferred_element_type=jnp.float32)
    weighted = logits * (window(span_z)[:, None, None] * window(span_x)[None, :, None])
    rest_z = core_z - margin
    rest_x = core_x - margin
    from_lower_x = from_behind(weighted[:, margin + core_x :], "xy", 1)
    from_upper_x = from_behind(weighted[:, :margin], "xy", -1)
    slab_rows = weighted[:, margin : margin + core_x]
    slab_rows = (
        slab_rows
        + place_at(from_lower_x, (0, 0), (0, rest_x))
        + place_at(from_upper_x, (0, 0), (rest_x, 0))
    )
    from_lower_z = from_behind(slab_rows[margin + core_z :], "gz", 1)
    from_upper_z = from_behind(slab_rows[:margin], "gz", -1)
    blended_sum = (
        slab_rows[margin : margin + core_z]
        + place_at(from_lower_z, (0, rest_z), (0, 0))
        + place_at(from_upper_z, (rest_z, 0), (0, 0))
    )
    cover_sum = (
        coverage(core_z, margin, lax.axis_index("gz"), lax.axis_size("gz"))[:, None, None]
        * coverage(core_x, margin, lax.axis_index("xy"), lax.axis_size("xy"))[None, :, None]
    )
    probability = jax.nn.sigmoid(blended_sum / cover_sum)
    extended = with_halo(probability, (("gz", 0), ("xy", 1)), RIM)
    vessel_sum = jnp.zeros_like(probability)
    for radius in (RIM // 4, RIM // 2, RIM):
        vessel_sum = vessel_sum + hessian_tube(extended, core_z, core_x, y_cells, radius)
    vesselness = VESSEL_GAIN * tissue_mask.astype(jnp.float32) * vessel_sum
    return (probability, vesselness)


def solution(mesh):
    placed = (P(None, "gz", "xy", None), P(), P(), P(), P(), P(), P("gz", "xy", None))
    return jax.shard_map(
        on_device,
        mesh=mesh,
        in_specs=placed,
        out_specs=(P("gz", "xy", None), P("gz", "xy", None)),
        check_vma=False,
    )
```

profile of v0, /device:TPU:247, one launch (start us, length us, event | category | flops | bytes accessed | tf_op | source)
XLA Modules:
  0.0 169.7 jit_solution(14901197658289139645)
XLA Ops:
  0.7 1.7 pad.40
  2.4 5.8 %reshape.100 = bf16[16,10,18,1,8,17]{5,4,0,2,1,3:T(8,128)(2,1)} reshape(bf16[16,10,18,1,136]{4,0,2,1,3:T(8,128)(2,1)S(1)} %pad.40) | data formatting | bytes 1566720 | tf_op jit(solution)/shard_map/conv_general_dilated | solution.py:39
  8.2 12.6 %copy.11 = bf16[16,10,18,1,8,17]{0,4,5,2,1,3:T(8,128)(2,1)} copy(bf16[16,10,18,1,8,17]{5,4,0,2,1,3:T(8,128)(2,1)} %reshape.100) | data formatting | bytes 1566720 | tf_op jit(solution)/shard_map/conv_general_dilated | solution.py:39
  20.8 1.3 slice.60
  22.2 17.1 %fusion.22 = bf16[10,18,1,8,17,16]{5,3,4,1,0,2:T(8,128)(2,1)S(1)} fusion(f32[16]{0:T(128)S(1)} %copy-done.5, pred[8,17]{0,1:T(8,128)(4,1)S(1)} %copy-done.6, bf16[16,16,3,3,3]{1,0,4,3,2:T(8,128)(2,1)S(1)} %copy-done, bf16[16,10,18,1,7,2]{0,4,5,2,1,3:T(8,128)(2,1)S(1)} %slice.60, bf16[16,10,18,1,8,17]{0,4,5,2,1,3:T(8,128)(2,1)} %copy.11), kind=kOutput, calls=%fused_computation.23 | convolution fusion | flops 308737536 | bytes 1661384 | tf_op jit(solution)/shard_map/conv_general_dilated | solution.py:39
  39.4 16.3 %fusion.5 = f32[10,18,8,17,16]{4,2,3,1,0:T(8,128)} fusion(bf16[16,16,3,3,3]{1,0,4,3,2:T(8,128)(2,1)S(1)} %copy-done.3, bf16[10,18,1,7,1,16]{5,3,4,1,0,2:T(8,128)(2,1)S(1)} %get-tuple-element.7, bf16[10,18,1,7,1,16]{5,3,4,1,0,2:T(8,128)(2,1)S(1)} %get-tuple-element.6, bf16[10,18,1,8,17,16]{5,3,4,1,0,2:T(8,128)(2,1)S(1)} %fusion.22), kind=kOutput, calls=%fused_computation.9 | convolution fusion | flops 308530176 | bytes 2444544 | tf_op jit(solution)/shard_map/conv_general_dilated | solution.py:39
  55.8 14.8 %copy.12 = f32[10,18,8,17,16]{3,2,4,1,0:T(8,128)} copy(f32[10,18,8,17,16]{4,2,3,1,0:T(8,128)} %fusion.5) | data formatting | bytes 3133440 | tf_op jit(solution)/shard_map/conv_general_dilated | solution.py:39
  70.6 7.8 %reshape.107 = f32[10,18,1,136,16]{3,4,1,0,2:T(8,128)S(1)} reshape(f32[10,18,8,17,16]{3,2,4,1,0:T(8,128)} %copy.12) | data formatting | bytes 3133440 | tf_op jit(solution)/shard_map/conv_general_dilated | solution.py:39
  78.9 2.8 %collective-permute-start = (f32[10,1,128]{2,0,1:T(8,128)S(1)}, f32[10,1,128]{2,0,1:T(8,128)S(1)}, u32[]{:S(2)}, u32[]{:S(2)}) collective-permute-start(f32[10,1,128]{2,0,1:T(8,128)S(1)} %get-tuple-element.10), channel_id=1, source_target_pairs={{0,1},{1,2},{2,3},{3,4},{4,5},{5,6},{6,7},{8,9},{9,10},{10,11},{11... | collective-permute-start | bytes 15368 | tf_op jit(solution)/shard_map/ppermute | solution.py:17
  81.7 2.5 %collective-permute-start.1 = (f32[10,1,128]{2,0,1:T(8,128)S(1)}, f32[10,1,128]{2,0,1:T(8,128)S(1)}, u32[]{:S(2)}, u32[]{:S(2)}) collective-permute-start(f32[10,1,128]{2,0,1:T(8,128)S(1)} %get-tuple-element.11), channel_id=1, source_target_pairs={{1,0},{2,1},{3,2},{4,3},{5,4},{6,5},{7,6},{9,8},{10,9},{11,10},{12... | collective-permute-start | bytes 15368 | tf_op jit(solution)/shard_map/ppermute | solution.py:17
  85.4 1.3 multiply_add_fusion.4
  86.7 1.4 multiply_add_fusion.3
  88.3 6.8 %collective-permute-start.2 = (f32[1,16,128]{2,0,1:T(1,128)S(1)}, f32[1,16,128]{2,0,1:T(1,128)S(1)}, u32[]{:S(2)}, u32[]{:S(2)}) collective-permute-start(f32[1,16,128]{2,0,1:T(1,128)S(1)} %get-tuple-element.12), channel_id=1, source_target_pairs={{0,8},{8,16},{16,24},{24,32},{32,40},{40,48},{48,56},{56,64},{64,7... | collective-permute-start | bytes 24584 | tf_op jit(solution)/shard_map/ppermute | solution.py:17
  95.1 1.9 %collective-permute-start.3 = (f32[1,16,128]{2,0,1:T(1,128)S(1)}, f32[1,16,128]{2,0,1:T(1,128)S(1)}, u32[]{:S(2)}, u32[]{:S(2)}) collective-permute-start(f32[1,16,128]{2,0,1:T(1,128)S(1)} %get-tuple-element.13), channel_id=1, source_target_pairs={{8,0},{16,8},{24,16},{32,24},{40,32},{48,40},{56,48},{64,56},{72,6... | collective-permute-start | bytes 24584 | tf_op jit(solution)/shard_map/ppermute | solution.py:17
  99.0 4.7 %collective-permute-done.3 = f32[1,16,128]{2,0,1:T(1,128)S(1)} collective-permute-done((f32[1,16,128]{2,0,1:T(1,128)S(1)}, f32[1,16,128]{2,0,1:T(1,128)S(1)}, u32[]{:S(2)}, u32[]{:S(2)}) %collective-permute-start.3) | collective-permute-done | bytes 8224 | tf_op jit(solution)/shard_map/ppermute | solution.py:17
  103.8 2.6 %collective-permute-start.4 = (f32[8,16,128]{2,0,1:T(8,128)S(1)}, f32[8,16,128]{2,0,1:T(8,128)S(1)}, u32[]{:S(2)}, u32[]{:S(2)}) collective-permute-start(f32[8,16,128]{2,0,1:T(8,128)S(1)} %fusion.62), channel_id=1, source_target_pairs={{0,8},{8,16},{16,24},{24,32},{32,40},{40,48},{48,56},{56,64},{64,7... | collective-permute-start | bytes 196616 | tf_op jit(solution)/shard_map/ppermute | solution.py:27
  106.3 1.9 %collective-permute-start.5 = (f32[8,16,128]{2,0,1:T(8,128)S(1)}, f32[8,16,128]{2,0,1:T(8,128)S(1)}, u32[]{:S(2)}, u32[]{:S(2)}) collective-permute-start(f32[8,16,128]{2,0,1:T(8,128)S(1)} %fusion.62), channel_id=1, source_target_pairs={{8,0},{16,8},{24,16},{32,24},{40,32},{48,40},{56,48},{64,56},{72,6... | collective-permute-start | bytes 196616 | tf_op jit(solution)/shard_map/ppermute | solution.py:28
  108.3 7.2 %collective-permute-done.5 = f32[8,16,128]{2,0,1:T(8,128)S(1)} collective-permute-done((f32[8,16,128]{2,0,1:T(8,128)S(1)}, f32[8,16,128]{2,0,1:T(8,128)S(1)}, u32[]{:S(2)}, u32[]{:S(2)}) %collective-permute-start.5) | collective-permute-done | bytes 65568 | tf_op jit(solution)/shard_map/ppermute | solution.py:28
  115.6 4.5 %collective-permute-start.6 = (f32[24,8,128]{2,0,1:T(8,128)S(1)}, f32[24,8,128]{2,0,1:T(8,128)S(1)}, u32[]{:S(2)}, u32[]{:S(2)}) collective-permute-start(f32[24,8,128]{2,0,1:T(8,128)S(1)} %get-tuple-element.8), channel_id=1, source_target_pairs={{0,1},{1,2},{2,3},{3,4},{4,5},{5,6},{6,7},{8,9},{9,10},{10,11},{11... | collective-permute-start | bytes 294920 | tf_op jit(solution)/shard_map/ppermute | solution.py:27
  120.1 2.1 %collective-permute-start.7 = (f32[24,8,128]{2,0,1:T(8,128)S(1)}, f32[24,8,128]{2,0,1:T(8,128)S(1)}, u32[]{:S(2)}, u32[]{:S(2)}) collective-permute-start(f32[24,8,128]{2,0,1:T(8,128)S(1)} %get-tuple-element.9), channel_id=1, source_target_pairs={{1,0},{2,1},{3,2},{4,3},{5,4},{6,5},{7,6},{9,8},{10,9},{11,10},{12... | collective-permute-start | bytes 294920 | tf_op jit(solution)/shard_map/ppermute | solution.py:28
  122.9 4.7 %collective-permute-done.7 = f32[24,8,128]{2,0,1:T(8,128)S(1)} collective-permute-done((f32[24,8,128]{2,0,1:T(8,128)S(1)}, f32[24,8,128]{2,0,1:T(8,128)S(1)}, u32[]{:S(2)}, u32[]{:S(2)}) %collective-permute-start.7) | collective-permute-done | bytes 98336 | tf_op jit(solution)/shard_map/ppermute | solution.py:28
  127.5 0.9 fusion.173
  128.5 0.8 convolution_bitcast_fusion.12
  130.1 0.8 convolution_bitcast_fusion.16
  131.0 0.9 fusion.155
  131.9 0.8 convolution_bitcast_fusion.14
  133.6 1.0 fusion.169
  134.6 0.9 convolution_bitcast_fusion.6
  135.5 0.9 convolution_bitcast_fusion.9
  136.5 0.9 convolution_bitcast_fusion.10
  137.4 1.1 fusion.159
  138.5 0.9 convolution_bitcast_fusion.8
  139.4 0.9 convolution_bitcast_fusion.7
  140.3 1.0 fusion.165
  141.3 0.9 convolution_bitcast_fusion.3
  142.2 0.9 convolution_bitcast_fusion.4
  143.1 0.9 convolution_bitcast_fusion
  144.0 1.0 fusion.163
  145.1 0.9 convolution_bitcast_fusion.2
  146.0 0.9 convolution_bitcast_fusion.1
  146.9 0.9 fusion.175
  147.8 0.8 convolution_bitcast_fusion.17
  148.7 0.8 convolution_multiply_fusion.17
  149.5 0.8 convolution_multiply_fusion.12
  150.3 0.8 convolution_multiply_fusion.15
  151.2 0.8 convolution_multiply_fusion.16
  152.0 0.8 convolution_multiply_fusion.14
  152.9 0.8 convolution_multiply_fusion.13
  153.7 1.0 fusion.171
  154.8 0.9 convolution_bitcast_fusion.11
  155.7 0.9 convolution_multiply_fusion.11
  156.6 0.9 convolution_multiply_fusion.6
  157.6 0.9 convolution_multiply_fusion.9
  158.5 0.9 convolution_multiply_fusion.10
  159.4 0.9 convolution_multiply_fusion.8
  160.3 0.9 convolution_multiply_fusion.7
  161.3 1.0 fusion.167
  162.3 0.9 convolution_bitcast_fusion.5
  163.2 0.9 convolution_multiply_fusion.5
  164.1 0.9 convolution_multiply_fusion.3
  165.1 0.9 convolution_multiply_fusion.4
  166.0 0.9 convolution_multiply_fusion.2
  166.9 0.9 convolution_multiply_fusion.1
  167.8 1.9 %add_multiply_fusion = f32[8,16,128]{2,1,0:T(8,128)} fusion(f32[8,16,128]{2,1,0:T(8,128)S(1)} %convolution_multiply_fusion.1, f32[8,16,128]{2,1,0:T(8,128)S(1)} %convolution_multiply_fusion.4, f32[8,16,128]{2,1,0:T(8,128)S(1)} %convolution_multiply_fusion.2, f32[8,16,128]{2,1,0:T(8,128)S(1)} %convolution_multiply_fusion.3, ...), kind=kOutput, calls=%fused_computation.134 | convolution fusion | flops 27017216 | bytes 1310724 | tf_op jit(solution)/shard_map/zxj,ij->zxi/dot_general | solution.py:125
  (42 shorter events, 6.5 us)
Async XLA Ops:
  0.6 21.5 %copy-start = (bf16[16,16,3,3,3]{1,0,4,3,2:T(8,128)(2,1)S(1)}, bf16[16,16,3,3,3]{1,0,4,3,2:T(8,128)(2,1)}, u32[]{:S(2)}) copy-start(bf16[16,16,3,3,3]{1,0,4,3,2:T(8,128)(2,1)} %param.8) | copy-start | bytes 41476
  8.2 14.0 %copy-start.5 = (f32[16]{0:T(128)S(1)}, f32[16]{0:T(128)}, u32[]{:S(2)}) copy-start(f32[16]{0:T(128)} %param.9) | copy-start | bytes 196
  8.2 14.0 %copy-start.6 = (pred[8,17]{0,1:T(8,128)(4,1)S(1)}, pred[8,17]{0,1:T(8,128)(4,1)}, u32[]{:S(2)}) copy-start(pred[8,17]{0,1:T(8,128)(4,1)} %constant.190) | copy-start | bytes 412
  22.2 17.2 %copy-start.3 = (bf16[16,16,3,3,3]{1,0,4,3,2:T(8,128)(2,1)S(1)}, bf16[16,16,3,3,3]{1,0,4,3,2:T(8,128)(2,1)}, u32[]{:S(2)}) copy-start(bf16[16,16,3,3,3]{1,0,4,3,2:T(8,128)(2,1)} %param.10) | copy-start | bytes 41476
  70.6 7.9 %copy-start.1 = (f32[16]{0:T(128)S(1)}, f32[16]{0:T(128)}, u32[]{:S(2)}) copy-start(f32[16]{0:T(128)} %param.11) | copy-start | bytes 196
  70.6 7.9 %copy-start.2 = (bf16[16]{0:T(256)(128)(2,1)S(1)}, bf16[16]{0:T(256)(128)(2,1)}, u32[]{:S(2)}) copy-start(bf16[16]{0:T(256)(128)(2,1)} %param.12) | copy-start | bytes 100
  78.9 9.1 %collective-permute-start = (f32[10,1,128]{2,0,1:T(8,128)S(1)}, f32[10,1,128]{2,0,1:T(8,128)S(1)}, u32[]{:S(2)}, u32[]{:S(2)}) collective-permute-start(f32[10,1,128]{2,0,1:T(8,128)S(1)} %get-tuple-element.10), channel_id=1, source_target_pairs={{0,1},{1,2},{2,3},{3,4},{4,5},{5,6},{6,7},{8,9},{9,10},{10,11},{11... | collective-permute-start | bytes 15368 | tf_op jit(solution)/shard_map/ppermute | solution.py:17
  81.7 6.5 %collective-permute-start.1 = (f32[10,1,128]{2,0,1:T(8,128)S(1)}, f32[10,1,128]{2,0,1:T(8,128)S(1)}, u32[]{:S(2)}, u32[]{:S(2)}) collective-permute-start(f32[10,1,128]{2,0,1:T(8,128)S(1)} %get-tuple-element.11), channel_id=1, source_target_pairs={{1,0},{2,1},{3,2},{4,3},{5,4},{6,5},{7,6},{9,8},{10,9},{11,10},{12... | collective-permute-start | bytes 15368 | tf_op jit(solution)/shard_map/ppermute | solution.py:17
  88.3 10.7 %collective-permute-start.2 = (f32[1,16,128]{2,0,1:T(1,128)S(1)}, f32[1,16,128]{2,0,1:T(1,128)S(1)}, u32[]{:S(2)}, u32[]{:S(2)}) collective-permute-start(f32[1,16,128]{2,0,1:T(1,128)S(1)} %get-tuple-element.12), channel_id=1, source_target_pairs={{0,8},{8,16},{16,24},{24,32},{32,40},{40,48},{48,56},{56,64},{64,7... | collective-permute-start | bytes 24584 | tf_op jit(solution)/shard_map/ppermute | solution.py:17
  95.1 8.6 %collective-permute-start.3 = (f32[1,16,128]{2,0,1:T(1,128)S(1)}, f32[1,16,128]{2,0,1:T(1,128)S(1)}, u32[]{:S(2)}, u32[]{:S(2)}) collective-permute-start(f32[1,16,128]{2,0,1:T(1,128)S(1)} %get-tuple-element.13), channel_id=1, source_target_pairs={{8,0},{16,8},{24,16},{32,24},{40,32},{48,40},{56,48},{64,56},{72,6... | collective-permute-start | bytes 24584 | tf_op jit(solution)/shard_map/ppermute | solution.py:17
  103.8 4.5 %collective-permute-start.4 = (f32[8,16,128]{2,0,1:T(8,128)S(1)}, f32[8,16,128]{2,0,1:T(8,128)S(1)}, u32[]{:S(2)}, u32[]{:S(2)}) collective-permute-start(f32[8,16,128]{2,0,1:T(8,128)S(1)} %fusion.62), channel_id=1, source_target_pairs={{0,8},{8,16},{16,24},{24,32},{32,40},{40,48},{48,56},{56,64},{64,7... | collective-permute-start | bytes 196616 | tf_op jit(solution)/shard_map/ppermute | solution.py:27
  106.3 9.2 %collective-permute-start.5 = (f32[8,16,128]{2,0,1:T(8,128)S(1)}, f32[8,16,128]{2,0,1:T(8,128)S(1)}, u32[]{:S(2)}, u32[]{:S(2)}) collective-permute-start(f32[8,16,128]{2,0,1:T(8,128)S(1)} %fusion.62), channel_id=1, source_target_pairs={{8,0},{16,8},{24,16},{32,24},{40,32},{48,40},{56,48},{64,56},{72,6... | collective-permute-start | bytes 196616 | tf_op jit(solution)/shard_map/ppermute | solution.py:28
  115.6 7.3 %collective-permute-start.6 = (f32[24,8,128]{2,0,1:T(8,128)S(1)}, f32[24,8,128]{2,0,1:T(8,128)S(1)}, u32[]{:S(2)}, u32[]{:S(2)}) collective-permute-start(f32[24,8,128]{2,0,1:T(8,128)S(1)} %get-tuple-element.8), channel_id=1, source_target_pairs={{0,1},{1,2},{2,3},{3,4},{4,5},{5,6},{6,7},{8,9},{9,10},{10,11},{11... | collective-permute-start | bytes 294920 | tf_op jit(solution)/shard_map/ppermute | solution.py:27
  120.1 7.5 %collective-permute-start.7 = (f32[24,8,128]{2,0,1:T(8,128)S(1)}, f32[24,8,128]{2,0,1:T(8,128)S(1)}, u32[]{:S(2)}, u32[]{:S(2)}) collective-permute-start(f32[24,8,128]{2,0,1:T(8,128)S(1)} %get-tuple-element.9), channel_id=1, source_target_pairs={{1,0},{2,1},{3,2},{4,3},{5,4},{6,5},{7,6},{9,8},{10,9},{11,10},{12... | collective-permute-start | bytes 294920 | tf_op jit(solution)/shard_map/ppermute | solution.py:28
  137.4 30.4 %copy-start.4 = (s32[8,16,128]{2,1,0:T(8,128)S(1)}, s32[8,16,128]{2,1,0:T(8,128)}, u32[]{:S(2)}) copy-start(s32[8,16,128]{2,1,0:T(8,128)} %param.13) | copy-start | bytes 196612
where the time goes:
time: 171 us; the launch traced here: 170 us
  matrix products  75.6 us (44%)
  local copies, waits for them, and re-layouts  46.1 us (27%)
  starting transfers between devices  25.1 us (15%)
  waiting for transfers between devices  16.8 us (10%)
  other arithmetic  4.91 us (3%)
    conv_general_dilated x5, local copies, waits for them, and re-layouts, conv_layer(): lax.conv_general_dilated(inputs[None], weight, (1, 1, 1), 'SAME', dimensi...  42.4 us
    conv_general_dilated x2, matrix products, conv_layer(): lax.conv_general_dilated(inputs[None], weight, (1, 1, 1), 'SAME', dimensi...  33.4 us
    dot_general x18, matrix products, pass_y(): jnp.einsum('zxj,ij->zxi', volume, band_matrix(y_cells, y_cells, 0, radius...  17.1 us
    dot_general x18, matrix products, pass_x(): jnp.einsum('ij,zjy->ziy', band_matrix(core_x, core_x + 2 * RIM, RIM, radi...  15.8 us
    ppermute x4, starting transfers between devices, from_behind(): return lax.ppermute(block, axis, route)  14 us
    ppermute x2, waiting for transfers between devices, with_halo(): after = lax.ppermute(initial, axis, down)  11.9 us
    dot_general x9, matrix products, pass_z(): jnp.einsum('ij,jxy->ixy', band_matrix(core_z, core_z + 2 * RIM, RIM, radi...  9 us
    ppermute x2, starting transfers between devices, with_halo(): before = lax.ppermute(last, axis, up)  7.02 us
  transfers between devices with their start and end apart: 8, of which 4 were waited for; matrix products, arithmetic and copies ran while one was open for 4% of the time, Pallas kernels for 0%

commit v1 on v0

v1 whole, which is shorter than its diff:
```python
import jax
import jax.numpy as jnp
import numpy as np
from jax import lax
from jax.experimental import pallas as pl
from jax.experimental.pallas import tpu as pltpu
from jax.sharding import PartitionSpec as P

CHANNELS = 16
CZ = 8
CX = 16
YC = 128
MARGIN = 1
RIM = 8
SPAN_Z = CZ + 2 * MARGIN
SPAN_X = CX + 2 * MARGIN
HALF = SPAN_X // 2
ROWS = SPAN_Z * CHANNELS
SLOT = 512
RADII = (RIM // 4, RIM // 2, RIM)
VESSEL_GAIN = 4.0
TUBE_FLOOR = 0.01
VMEM_LIMIT = 40 * 1024 * 1024


def window(size):
    position = np.arange(size, dtype=np.float64)
    return np.exp(-0.5 * ((position - (size - 1) / 2.0) / (size / 4.0)) ** 2)


WINDOW_Z = window(SPAN_Z)
WINDOW_X = window(SPAN_X)


def taps(radius, degree):
    spread = radius / 3.0
    offsets = np.arange(-radius, radius + 1, dtype=np.float64)
    gaussian = np.exp(-offsets * offsets / (2.0 * spread * spread))
    gaussian = gaussian / gaussian.sum()
    if degree == 1:
        return -offsets / spread**2 * gaussian
    if degree == 2:
        return (offsets**2 / spread**4 - 1.0 / spread**2) * gaussian
    return gaussian


def band(out_len, in_len, offset, radius, degree):
    weights = taps(radius, degree)
    distance = np.arange(out_len)[:, None] + offset - np.arange(in_len)[None, :]
    inside = np.abs(distance) <= radius
    return np.where(inside, weights[np.clip(distance, -radius, radius) + radius], 0.0)


def split_terms(matrix):
    whole = matrix.astype(np.float32)
    upper = whole.astype(jnp.bfloat16)
    lower = (whole - upper.astype(np.float32)).astype(jnp.bfloat16)
    return upper, lower


def filter_constants():
    x_upper, x_lower, y_all = [], [], []
    for radius in RADII:
        blocks = [
            np.kron(np.eye(CZ), band(CX, CX + 2 * RIM, RIM, radius, degree)) for degree in range(3)
        ]
        upper, lower = split_terms(np.concatenate(blocks, axis=0))
        x_upper.append(upper)
        x_lower.append(lower)
        for degree in range(3):
            scaled = (radius / 3.0) ** 2 * band(YC, YC, 0, radius, degree).T
            upper, lower = split_terms(scaled)
            top = np.concatenate([upper, lower], axis=1)
            bottom = np.concatenate([upper, np.zeros_like(lower)], axis=1)
            y_all.append(np.concatenate([top, bottom], axis=0))
    return np.stack(x_upper), np.stack(x_lower), np.stack(y_all)


def iota(shape, dim):
    return lax.broadcasted_iota(jnp.int32, shape, dim)


def y_neighbours(values):
    lane = iota(values.shape, 1)
    before = jnp.where(lane == 0, 0.0, pltpu.roll(values, 1, 1))
    after = jnp.where(lane == YC - 1, 0.0, pltpu.roll(values, YC - 1, 1))
    return (before, values, after)


def store_column(slots_ref, slot, half, three):
    lanes = pl.ds(half * YC, YC)
    for dy in range(3):
        slots_ref[pl.ds(slot * SLOT + dy * ROWS, ROWS), lanes] = three[dy]


def expand_weight(weight_ref, wide_ref):
    lane = iota((CHANNELS, SLOT), 1)
    group = (lane >= ROWS).astype(jnp.int32) + (lane >= 2 * ROWS).astype(jnp.int32) + (
        lane >= 3 * ROWS
    ).astype(jnp.int32)
    row = iota((CHANNELS, SLOT), 0)
    same = (lane & (CHANNELS - 1)) == row
    spread = jnp.zeros((9 * CHANNELS, SLOT), jnp.float32)
    for dy in range(3):
        pick = jnp.where(same & (group == dy), 1.0, 0.0).astype(jnp.bfloat16)
        part = weight_ref[:, :, dy].reshape(9 * CHANNELS, CHANNELS)
        spread = spread + jnp.dot(part, pick, preferred_element_type=jnp.float32)
    plane = (lane - group * ROWS) >> 4
    for dx in range(3):
        three = [
            spread[(dz * 3 + dx) * CHANNELS : (dz * 3 + dx + 1) * CHANNELS] for dz in range(3)
        ]
        for z in range(SPAN_Z):
            rows = jnp.where(
                plane == z - 1,
                three[0],
                jnp.where(plane == z, three[1], jnp.where(plane == z + 1, three[2], 0.0)),
            )
            wide_ref[z * CHANNELS : (z + 1) * CHANNELS, dx * SLOT : (dx + 1) * SLOT] = rows.astype(
                jnp.bfloat16
            )


def column_of(row_ref):
    eye = iota((CHANNELS, CHANNELS), 0) == iota((CHANNELS, CHANNELS), 1)
    return jnp.sum(jnp.where(eye, row_ref[...], 0.0), axis=1, keepdims=True)


def decoder_kernel(
    features_ref,
    weight1_ref,
    bias1_ref,
    weight2_ref,
    bias2_ref,
    head_ref,
    patch_ref,
    low_ref,
    high_ref,
    first_ref,
    second_ref,
    wide1_ref,
    wide2_ref,
):
    expand_weight(weight1_ref, wide1_ref)
    expand_weight(weight2_ref, wide2_ref)
    for ref in (first_ref, second_ref):
        ref[0:SLOT, 0:YC] = jnp.zeros((SLOT, YC), jnp.bfloat16)
        ref[(HALF + 1) * SLOT :, YC:] = jnp.zeros((SLOT, YC), jnp.bfloat16)
        for slot in range(HALF + 2):
            ref[slot * SLOT + 3 * ROWS : (slot + 1) * SLOT, :] = jnp.zeros(
                (SLOT - 3 * ROWS, 2 * YC), jnp.bfloat16
            )
    for x in range(SPAN_X):
        column = features_ref[:, x].reshape(ROWS, YC).astype(jnp.float32)
        three = [v.astype(jnp.bfloat16) for v in y_neighbours(column)]
        if x <= HALF:
            store_column(first_ref, x + 1, 0, three)
        if x >= HALF - 1:
            store_column(first_ref, x - HALF + 1, 1, three)

    def layer(wide_ref, slots_ref, bias, step):
        summed = jnp.dot(
            wide_ref[...],
            slots_ref[step * SLOT : (step + 3) * SLOT, :],
            preferred_element_type=jnp.float32,
        )
        shaped = summed.reshape(SPAN_Z, CHANNELS, 2 * YC) + bias[None]
        return jnp.maximum(shaped, 0.0).reshape(ROWS, 2 * YC)

    bias1 = column_of(bias1_ref)
    for step in range(HALF):
        hidden = layer(wide1_ref, first_ref, bias1, step)
        for half in range(2):
            part = hidden[:, half * YC : (half + 1) * YC]
            three = [v.astype(jnp.bfloat16) for v in y_neighbours(part)]
            store_column(second_ref, step + 1, half, three)
            if half == 0 and step == HALF - 1:
                store_column(second_ref, 0, 1, three)
            if half == 1 and step == 0:
                store_column(second_ref, HALF + 1, 0, three)

    bias2 = column_of(bias2_ref)
    repeat = ((iota((CHANNELS, ROWS), 1) & (CHANNELS - 1)) == iota((CHANNELS, ROWS), 0)).astype(
        jnp.float32
    )
    head_lanes = jnp.sum(
        repeat * column_of(head_ref), axis=0, keepdims=True
    )
    head = jnp.where(
        (iota((16, ROWS), 1) >> 4) == iota((16, ROWS), 0), head_lanes, 0.0
    ).astype(jnp.bfloat16)
    place = iota((16, YC), 0).astype(jnp.float32)
    centred = (place - (SPAN_Z - 1) / 2.0) / (SPAN_Z / 4.0)
    weight_z = jnp.exp(-0.5 * centred * centred)
    low_ref[16:24] = jnp.zeros((8, YC), jnp.float32)
    high_ref[16:24] = jnp.zeros((8, YC), jnp.float32)
    for step in range(HALF):
        hidden = layer(wide2_ref, second_ref, bias2, step).astype(jnp.bfloat16)
        logits = jnp.dot(head, hidden, preferred_element_type=jnp.float32)
        for half in range(2):
            x = step + half * HALF
            weighted = logits[:, half * YC : (half + 1) * YC] * (weight_z * float(WINDOW_X[x]))
            if x == 0 or x == SPAN_X - 1:
                side = 0 if x == 0 else 1
                patch_ref[160 + side * 16 : 176 + side * 16, :] = weighted
                row = 16 + side
            else:
                patch_ref[pl.ds(x - 1, SPAN_Z, stride=CX), :] = weighted[:SPAN_Z]
                row = x - 1
            low_ref[row : row + 1, :] = weighted[0:1]
            high_ref[row : row + 1, :] = weighted[SPAN_Z - 1 : SPAN_Z]


def slab_kernel(below_ref, own_ref, above_ref, far_below_ref, far_above_ref, left_ref, right_ref):
    refs = (below_ref, own_ref, above_ref)
    row = iota((CZ, YC), 0)
    for block in range(3):
        ref = refs[block]
        for i in range(CZ):
            value = ref[(i + 1) * CX : (i + 2) * CX, :]
            if i == 0:
                if block == 0:
                    value = value + far_below_ref[0:CX]
                else:
                    value = value + refs[block - 1][9 * CX : 10 * CX, :]
            if i == CZ - 1:
                if block == 2:
                    value = value + far_above_ref[0:CX]
                else:
                    value = value + refs[block + 1][0:CX, :]
            z = block * CZ + i
            left_ref[z * 8 : (z + 1) * 8, :] = value[:8]
            right_ref[z * 8 : (z + 1) * 8, :] = value[8:]
        for side, out_ref in enumerate((left_ref, right_ref)):
            base = 160 + side * 16
            value = ref[base + 1 : base + 9, :]
            if block == 0:
                lower = far_below_ref[16 + side : 17 + side]
            else:
                lower = refs[block - 1][base + 9 : base + 10, :]
            if block == 2:
                upper = far_above_ref[16 + side : 17 + side]
            else:
                upper = refs[block + 1][base : base + 1, :]
            value = value + jnp.where(row == 0, lower, 0.0) + jnp.where(row == CZ - 1, upper, 0.0)
            out_ref[192 + block * 8 : 200 + block * 8, :] = value


def two_terms(values):
    upper = values.astype(jnp.bfloat16)
    lower = (values - upper.astype(jnp.float32)).astype(jnp.bfloat16)
    return upper, lower


def vessel_kernel(
    place_ref,
    left_ref,
    right_ref,
    from_left_ref,
    from_right_ref,
    tissue_ref,
    x_upper_ref,
    x_lower_ref,
    y_ref,
    probability_ref,
    vessel_ref,
    extended_ref,
    along_z_ref,
):
    at_z, count_z, at_x, count_x = (place_ref[k] for k in range(4))
    sub = iota((8, YC), 0)

    def inverse_x(first, edge, edge_row, present):
        cover = jnp.zeros((8, YC), jnp.float32)
        for j in range(8):
            cover = jnp.where(sub == j, float(WINDOW_X[first + j + 1]), cover)
        extra = jnp.where(present, float(edge), 0.0)
        return 1.0 / (cover + jnp.where(sub == edge_row, extra, 0.0))

    wx_last, wx_first = WINDOW_X[SPAN_X - 1], WINDOW_X[0]
    yes = at_x >= 0
    inverse = [
        inverse_x(8, wx_first, 7, yes),
        inverse_x(0, wx_last, 0, at_x > 0),
        inverse_x(8, wx_first, 7, at_x < count_x - 1),
        inverse_x(0, wx_last, 0, yes),
    ]
    wz_last, wz_first = WINDOW_Z[SPAN_Z - 1], WINDOW_Z[0]
    lower_there = (at_z > 1, at_z > 0, yes)
    upper_there = (yes, at_z < count_z - 1, at_z < count_z - 2)
    inside_x = (at_x > 0, yes, yes, at_x < count_x - 1)
    inside_z = (at_z > 0, yes, at_z < count_z - 1)
    keep_x = [jnp.where(flag, 1.0, 0.0) for flag in inside_x]
    keep_z = [jnp.where(flag, 1.0, 0.0) for flag in inside_z]
    for z in range(3 * CZ):
        block, i = divmod(z, CZ)
        plain = WINDOW_Z[i + 1]
        scale = float(1.0 / plain)
        if i == 0:
            scale = jnp.where(lower_there[block], float(1.0 / (plain + wz_last)), scale)
        if i == CZ - 1:
            scale = jnp.where(upper_there[block], float(1.0 / (plain + wz_first)), scale)
        rows = slice(z * 8, (z + 1) * 8)
        edge = slice(192 + z, 193 + z)
        sums = (
            from_left_ref[rows, :] + jnp.where(sub == 7, left_ref[edge, :], 0.0),
            left_ref[rows, :] + jnp.where(sub == 0, from_left_ref[edge, :], 0.0),
            right_ref[rows, :] + jnp.where(sub == 7, from_right_ref[edge, :], 0.0),
            from_right_ref[rows, :] + jnp.where(sub == 0, right_ref[edge, :], 0.0),
        )
        for k in range(4):
            value = 1.0 / (1.0 + jnp.exp(-(sums[k] * (inverse[k] * scale))))
            if block == 1 and k in (1, 2):
                at = i * CX + (k - 1) * 8
                probability_ref[at : at + 8, :] = value
            else:
                value = value * (keep_x[k] * keep_z[block])
            extended_ref[z * 32 + k * 8 : z * 32 + k * 8 + 8, :] = value

    weights = [[taps(radius, degree) for degree in range(3)] for radius in RADII]

    def one_plane(i, carry):
        def plane(offset):
            return extended_ref[pl.ds(pl.multiple_of((i + RIM + offset) * 32, 32), 32), :]

        centre = plane(0)
        results = {}
        for n, radius in enumerate(RADII):
            for degree in (0, 2):
                results[n, degree] = centre * float(weights[n][degree][radius])
        for k in range(1, RIM + 1):
            before, after = plane(-k), plane(k)
            both, change = before + after, before - after
            for n, radius in enumerate(RADII):
                if k > radius:
                    continue
                for degree in range(3):
                    term = (change if degree == 1 else both) * float(weights[n][degree][radius + k])
                    if (n, degree) in results:
                        results[n, degree] = results[n, degree] + term
                    else:
                        results[n, degree] = term
        for n in range(3):
            for degree in range(3):
                upper, lower = two_terms(results[n, degree])
                rows = pl.ds(pl.multiple_of((n * 3 + degree) * 256 + i * 32, 32), 32)
                along_z_ref[rows, 0:YC] = upper
                along_z_ref[rows, YC : 2 * YC] = lower
        return carry

    lax.fori_loop(0, CZ, one_plane, 0)

    total = jnp.zeros((CZ * CX, YC), jnp.float32)
    for n in range(3):
        after_x = {}
        for degree in range(3):
            count = (3 - degree) * 128
            data = along_z_ref[(n * 3 + degree) * 256 : (n * 3 + degree + 1) * 256, :]
            wide = jnp.dot(x_upper_ref[n, :count], data, preferred_element_type=jnp.float32)
            narrow = jnp.dot(
                x_lower_ref[n, :count], data[:, :YC], preferred_element_type=jnp.float32
            )
            summed = wide[:, :YC] + wide[:, YC:] + narrow
            for other in range(3 - degree):
                after_x[degree, other] = summed[other * 128 : (other + 1) * 128]

        def along_y(degree, keys):
            stacked = jnp.concatenate([after_x[key] for key in keys], axis=0)
            pair = jnp.concatenate(two_terms(stacked), axis=1)
            wide = jnp.dot(pair, y_ref[n * 3 + degree], preferred_element_type=jnp.float32)
            summed = wide[:, :YC] + wide[:, YC:]
            return [summed[at * 128 : (at + 1) * 128] for at in range(len(keys))]

        hzz, hxx, hzx = along_y(0, ((2, 0), (0, 2), (1, 1)))
        hzy, hxy = along_y(1, ((1, 0), (0, 1)))
        (hyy,) = along_y(2, ((0, 0),))
        first_inv = hzz + hxx + hyy
        second_inv = hzz * hxx + hzz * hyy + hxx * hyy - hzx * hzx - hzy * hzy - hxy * hxy
        third_inv = (
            hzz * (hxx * hyy - hxy * hxy)
            - hzx * (hzx * hyy - hxy * hzy)
            + hzy * (hzx * hxy - hxx * hzy)
        )
        positive = jnp.maximum(second_inv, 0.0)
        size = jnp.abs(third_inv)
        root = jnp.where(size > 0.0, jnp.exp(jnp.log(size) * (2.0 / 3.0)), 0.0)
        total = total + jnp.maximum(-first_inv, 0.0) * positive / (positive + root + TUBE_FLOOR)
    vessel_ref[...] = VESSEL_GAIN * tissue_ref[...].astype(jnp.float32) * total


def from_behind(block, axis, distance):
    devices = range(lax.axis_size(axis))
    route = [(i - distance, i) for i in devices if i - distance in devices]
    return lax.ppermute(block, axis, route)


def whole(count):
    return [pl.BlockSpec(memory_space=pltpu.VMEM)] * count


def on_device(
    patch_features, conv1_weight, conv1_bias, conv2_weight, conv2_bias, head_weight, tissue_mask
):
    f32 = jnp.float32
    params = pltpu.CompilerParams(vmem_limit_bytes=VMEM_LIMIT)
    patch, low, high = pl.pallas_call(
        decoder_kernel,
        out_shape=(
            jax.ShapeDtypeStruct((192, YC), f32),
            jax.ShapeDtypeStruct((24, YC), f32),
            jax.ShapeDtypeStruct((24, YC), f32),
        ),
        in_specs=whole(6),
        out_specs=tuple(whole(3)),
        scratch_shapes=[
            pltpu.VMEM(((HALF + 2) * SLOT, 2 * YC), jnp.bfloat16),
            pltpu.VMEM(((HALF + 2) * SLOT, 2 * YC), jnp.bfloat16),
            pltpu.VMEM((ROWS, 3 * SLOT), jnp.bfloat16),
            pltpu.VMEM((ROWS, 3 * SLOT), jnp.bfloat16),
        ],
        compiler_params=params,
        name="decoder",
    )(
        patch_features.transpose(1, 2, 0, 3),
        conv1_weight.transpose(2, 3, 4, 0, 1),
        conv1_bias.reshape(1, CHANNELS),
        conv2_weight.transpose(2, 3, 4, 0, 1),
        conv2_bias.reshape(1, CHANNELS),
        head_weight.astype(f32).reshape(1, CHANNELS),
    )
    below = from_behind(patch, "gz", 1)
    above = from_behind(patch, "gz", -1)
    far_below = from_behind(high, "gz", 2)
    far_above = from_behind(low, "gz", -2)
    left, right = pl.pallas_call(
        slab_kernel,
        out_shape=(
            jax.ShapeDtypeStruct((216, YC), f32),
            jax.ShapeDtypeStruct((216, YC), f32),
        ),
        in_specs=whole(5),
        out_specs=tuple(whole(2)),
        compiler_params=params,
        name="slab",
    )(below, patch, above, far_below, far_above)
    from_left = from_behind(right, "xy", 1)
    from_right = from_behind(left, "xy", -1)
    place = jnp.stack(
        [
            lax.axis_index("gz"),
            jnp.int32(lax.axis_size("gz")),
            lax.axis_index("xy"),
            jnp.int32(lax.axis_size("xy")),
        ]
    ).astype(jnp.int32)
    x_upper, x_lower, y_all = filter_constants()
    probability, vesselness = pl.pallas_call(
        vessel_kernel,
        out_shape=(
            jax.ShapeDtypeStruct((CZ * CX, YC), f32),
            jax.ShapeDtypeStruct((CZ * CX, YC), f32),
        ),
        in_specs=[pl.BlockSpec(memory_space=pltpu.SMEM)] + whole(8),
        out_specs=tuple(whole(2)),
        scratch_shapes=[
            pltpu.VMEM((3 * CZ * 32, YC), f32),
            pltpu.VMEM((9 * 256, 2 * YC), jnp.bfloat16),
        ],
        compiler_params=params,
        name="vessel",
    )(
        place,
        left,
        right,
        from_left,
        from_right,
        tissue_mask.reshape(CZ * CX, YC),
        jnp.asarray(x_upper),
        jnp.asarray(x_lower),
        jnp.asarray(y_all),
    )
    return (
        probability.reshape(CZ, CX, YC),
        vesselness.reshape(CZ, CX, YC),
    )


def solution(mesh):
    placed = (P(None, "gz", "xy", None), P(), P(), P(), P(), P(), P("gz", "xy", None))
    return jax.shard_map(
        on_device,
        mesh=mesh,
        in_specs=placed,
        out_specs=(P("gz", "xy", None), P("gz", "xy", None)),
        check_vma=False,
    )
```

time: 171 us -> 50.7 us (0.30)
  the two profiles are of different devices: /device:TPU:247 before, /device:TPU:120 now
where the time goes in v1:
time: 50.7 us; the launch traced here: 50.2 us
  starting transfers between devices  19.5 us (38%)
  waiting for transfers between devices  14 us (28%)
  Pallas kernels  8.82 us (17%)
  local copies, waits for them, and re-layouts  6.36 us (13%)
  other arithmetic  0.83 us (2%)
  between operations  0.72 us (1%)
    ppermute x6, starting transfers between devices, from_behind(): return lax.ppermute(block, axis, route)  19.5 us
    ppermute x6, waiting for transfers between devices, from_behind(): return lax.ppermute(block, axis, route)  14 us
    unnamed x18, local copies, waits for them, and re-layouts  6.36 us
    pallas_call x1, Pallas kernels, on_device(): pl.pallas_call(decoder_kernel, out_shape=(jax.ShapeDtypeStruct((192, YC),...  5.27 us
    pallas_call x1, Pallas kernels, on_device(): pl.pallas_call(vessel_kernel, out_shape=(jax.ShapeDtypeStruct((CZ * CX, Y...  3.53 us
  transfers between devices with their start and end apart: 6, of which 3 were waited for; matrix products, arithmetic and copies ran while one was open for 0% of the time, Pallas kernels for 0%

profile of v1, /device:TPU:120, one launch (start us, length us, event | category | flops | bytes accessed | tf_op | source)
XLA Modules:
  0.0 50.2 jit_solution(1495636497359737698)
XLA Ops:
  0.6 0.0 copy-start
  0.6 0.8 %bitcast_convert_fusion.head_ref = f32[1,16]{1,0:T(1,128)S(1)} fusion(bf16[16]{0:T(256)(128)(2,1)} %param.15), kind=kLoop, calls=%fused_computation.1 | loop fusion | flops 16 | bytes 96 | tf_op jit(solution)/shard_map/reshape | solution.py:429
  1.4 0.0 copy-start.1
  1.4 1.1 %copy-done.1 = bf16[16,10,18,128]{3,0,2,1:T(8,128)(2,1)S(1)} copy-done((bf16[16,10,18,128]{3,0,2,1:T(8,128)(2,1)S(1)}, bf16[16,10,18,128]{3,0,2,1:T(8,128)(2,1)}, u32[]{:S(2)}) %copy-start.1) | copy-done | bytes 737304
  2.5 0.0 copy-start.4
  2.5 0.9 %copy-done.4 = bf16[16,16,3,3,3]{1,0,4,3,2:T(8,128)(2,1)S(1)} copy-done((bf16[16,16,3,3,3]{1,0,4,3,2:T(8,128)(2,1)S(1)}, bf16[16,16,3,3,3]{1,0,4,3,2:T(8,128)(2,1)}, u32[]{:S(2)}) %copy-start.4) | copy-done | bytes 13848
  3.4 0.0 copy-start.5
  3.4 0.9 %copy-done.5 = bf16[16,16,3,3,3]{1,0,4,3,2:T(8,128)(2,1)S(1)} copy-done((bf16[16,16,3,3,3]{1,0,4,3,2:T(8,128)(2,1)S(1)}, bf16[16,16,3,3,3]{1,0,4,3,2:T(8,128)(2,1)}, u32[]{:S(2)}) %copy-start.5) | copy-done | bytes 13848
  4.3 0.0 copy-start.7
  4.3 0.7 %copy-done.7 = f32[16]{0:T(128)S(1)} copy-done((f32[16]{0:T(128)S(1)}, f32[16]{0:T(128)}, u32[]{:S(2)}) %copy-start.7) | copy-done | bytes 88
  5.0 0.0 copy-start.8
  5.0 0.7 %copy-done.8 = f32[16]{0:T(128)S(1)} copy-done((f32[16]{0:T(128)S(1)}, f32[16]{0:T(128)}, u32[]{:S(2)}) %copy-start.8) | copy-done | bytes 88
  5.6 0.0 copy-start.6
  5.6 5.3 %decoder.1 = (f32[192,128]{1,0:T(8,128)S(1)}, f32[24,128]{1,0:T(8,128)S(1)}, f32[24,128]{1,0:T(8,128)S(1)}) custom-call(bf16[10,18,16,128]{3,2,1,0:T(8,128)(2,1)S(1)} %bitcast.13, bf16[3,3,3,16,16]{4,3,2,1,0:T(8,128)(2,1)S(1)} %bitcast.14, f32[1,16]{1,0:T(1,128)S(1)} %bitcast.17, bf16[3,3,3,16,16]{4,3,2,1,0:T(8,128)(2,1)S(1)} %bitcast.15, ...), custom_call_target="tpu_custom_call" | custom-call | tf_op jit(solution)/shard_map/decoder/pallas_call | solution.py:406
  10.9 2.6 %collective-permute-start.1 = (f32[192,128]{1,0:T(8,128)S(1)}, f32[192,128]{1,0:T(8,128)S(1)}, u32[]{:S(2)}, u32[]{:S(2)}) collective-permute-start(f32[192,128]{1,0:T(8,128)S(1)} %get-tuple-element.9.own_ref), channel_id=1, source_target_pairs={{8,0},{16,8},{24,16},{32,24},{40,32},{48,40},{56,48},{64,56},{72,6... | collective-permute-start | bytes 294920 | tf_op jit(solution)/shard_map/ppermute | solution.py:394
  13.5 1.9 %collective-permute-start = (f32[192,128]{1,0:T(8,128)S(1)}, f32[192,128]{1,0:T(8,128)S(1)}, u32[]{:S(2)}, u32[]{:S(2)}) collective-permute-start(f32[192,128]{1,0:T(8,128)S(1)} %get-tuple-element.9.own_ref), channel_id=1, source_target_pairs={{0,8},{8,16},{16,24},{24,32},{32,40},{40,48},{48,56},{56,64},{64,7... | collective-permute-start | bytes 294920 | tf_op jit(solution)/shard_map/ppermute | solution.py:394
  15.4 6.3 %collective-permute-start.2 = (f32[24,128]{1,0:T(8,128)S(1)}, f32[24,128]{1,0:T(8,128)S(1)}, u32[]{:S(2)}, u32[]{:S(2)}) collective-permute-start(f32[24,128]{1,0:T(8,128)S(1)} %get-tuple-element.10), channel_id=1, source_target_pairs={{0,16},{8,24},{16,32},{24,40},{32,48},{40,56},{48,64},{56,72},{64,... | collective-permute-start | bytes 36872 | tf_op jit(solution)/shard_map/ppermute | solution.py:394
  21.7 1.9 %collective-permute-start.3 = (f32[24,128]{1,0:T(8,128)S(1)}, f32[24,128]{1,0:T(8,128)S(1)}, u32[]{:S(2)}, u32[]{:S(2)}) collective-permute-start(f32[24,128]{1,0:T(8,128)S(1)} %get-tuple-element.11), channel_id=1, source_target_pairs={{16,0},{24,8},{32,16},{40,24},{48,32},{56,40},{64,48},{72,56},{80,... | collective-permute-start | bytes 36872 | tf_op jit(solution)/shard_map/ppermute | solution.py:394
  23.7 0.0 collective-permute-done.2.far_below_ref
  23.7 7.3 %collective-permute-done.3.far_above_ref = f32[24,128]{1,0:T(8,128)S(1)} collective-permute-done((f32[24,128]{1,0:T(8,128)S(1)}, f32[24,128]{1,0:T(8,128)S(1)}, u32[]{:S(2)}, u32[]{:S(2)}) %collective-permute-start.3) | collective-permute-done | bytes 12320 | tf_op jit(solution)/shard_map/ppermute | solution.py:394
  30.9 0.0 collective-permute-done.1.above_ref
  30.9 0.0 collective-permute-done.below_ref
  31.0 4.9 %collective-permute-start.5 = (f32[216,128]{1,0:T(8,128)S(1)}, f32[216,128]{1,0:T(8,128)S(1)}, u32[]{:S(2)}, u32[]{:S(2)}) collective-permute-start(f32[216,128]{1,0:T(8,128)S(1)} %get-tuple-element.12.left_ref), channel_id=1, source_target_pairs={{1,0},{2,1},{3,2},{4,3},{5,4},{6,5},{7,6},{9,8},{10,9},{11,10},{12... | collective-permute-start | bytes 331784 | tf_op jit(solution)/shard_map/ppermute | solution.py:394
  35.8 1.9 %collective-permute-start.4 = (f32[216,128]{1,0:T(8,128)S(1)}, f32[216,128]{1,0:T(8,128)S(1)}, u32[]{:S(2)}, u32[]{:S(2)}) collective-permute-start(f32[216,128]{1,0:T(8,128)S(1)} %get-tuple-element.13.right_ref), channel_id=1, source_target_pairs={{0,1},{1,2},{2,3},{3,4},{4,5},{5,6},{6,7},{8,9},{9,10},{10,11},{11... | collective-permute-start | bytes 331784 | tf_op jit(solution)/shard_map/ppermute | solution.py:394
  37.8 0.1 pad_add_fusion.place_ref
  37.8 0.4 collective-permute-done.5.from_right_ref
  38.3 6.3 %collective-permute-done.4.from_left_ref = f32[216,128]{1,0:T(8,128)S(1)} collective-permute-done((f32[216,128]{1,0:T(8,128)S(1)}, f32[216,128]{1,0:T(8,128)S(1)}, u32[]{:S(2)}, u32[]{:S(2)}) %collective-permute-start.4) | collective-permute-done | bytes 110624 | tf_op jit(solution)/shard_map/ppermute | solution.py:394
  44.6 0.0 copy-done
  44.6 0.0 copy-done.6
  44.6 0.0 copy-start.2
  44.6 1.1 %copy-done.2 = bf16[3,384,256]{2,1,0:T(8,128)(2,1)S(1)} copy-done((bf16[3,384,256]{2,1,0:T(8,128)(2,1)S(1)}, bf16[3,384,256]{2,1,0:T(8,128)(2,1)}, u32[]{:S(2)}) %copy-start.2) | copy-done | bytes 589848
  45.6 0.0 copy-start.3
  45.6 1.1 %copy-done.3 = bf16[3,384,256]{2,1,0:T(8,128)(2,1)S(1)} copy-done((bf16[3,384,256]{2,1,0:T(8,128)(2,1)S(1)}, bf16[3,384,256]{2,1,0:T(8,128)(2,1)}, u32[]{:S(2)}) %copy-start.3) | copy-done | bytes 589848
  46.7 3.5 %vessel.1 = (f32[128,128]{1,0:T(8,128)}, f32[128,128]{1,0:T(8,128)}) custom-call(s32[4]{0:T(128)S(1)} %pad_add_fusion.place_ref, f32[216,128]{1,0:T(8,128)S(1)} %get-tuple-element.12.left_ref, f32[216,128]{1,0:T(8,128)S(1)} %get-tuple-element.13.right_ref, f32[216,128]{1,0:T(8,128)S(1)} %collective-permute-done.4.from_left_ref, ...), custom_call_target="tpu_custom_call" | custom-call | tf_op jit(solution)/shard_map/vessel/pallas_call | solution.py:457
  (1 shorter events, 0.0 us)
Async XLA Ops:
  0.6 43.9 %copy-start = (bf16[9,256,256]{2,1,0:T(8,128)(2,1)S(1)}, bf16[9,256,256]{2,1,0:T(8,128)(2,1)}, u32[]{:S(2)}) copy-start(bf16[9,256,256]{2,1,0:T(8,128)(2,1)} %constant.21.clone.y_ref) | copy-start | bytes 3538948
  1.4 1.1 %copy-start.1 = (bf16[16,10,18,128]{3,0,2,1:T(8,128)(2,1)S(1)}, bf16[16,10,18,128]{3,0,2,1:T(8,128)(2,1)}, u32[]{:S(2)}) copy-start(bf16[16,10,18,128]{3,0,2,1:T(8,128)(2,1)} %param.10) | copy-start | bytes 2211844
  2.5 0.9 %copy-start.4 = (bf16[16,16,3,3,3]{1,0,4,3,2:T(8,128)(2,1)S(1)}, bf16[16,16,3,3,3]{1,0,4,3,2:T(8,128)(2,1)}, u32[]{:S(2)}) copy-start(bf16[16,16,3,3,3]{1,0,4,3,2:T(8,128)(2,1)} %param.11) | copy-start | bytes 41476
  3.4 0.9 %copy-start.5 = (bf16[16,16,3,3,3]{1,0,4,3,2:T(8,128)(2,1)S(1)}, bf16[16,16,3,3,3]{1,0,4,3,2:T(8,128)(2,1)}, u32[]{:S(2)}) copy-start(bf16[16,16,3,3,3]{1,0,4,3,2:T(8,128)(2,1)} %param.13) | copy-start | bytes 41476
  4.3 0.7 %copy-start.7 = (f32[16]{0:T(128)S(1)}, f32[16]{0:T(128)}, u32[]{:S(2)}) copy-start(f32[16]{0:T(128)} %param.12) | copy-start | bytes 196
  5.0 0.7 %copy-start.8 = (f32[16]{0:T(128)S(1)}, f32[16]{0:T(128)}, u32[]{:S(2)}) copy-start(f32[16]{0:T(128)} %param.14) | copy-start | bytes 196
  5.6 39.0 %copy-start.6 = (s32[8,16,128]{2,1,0:T(8,128)S(1)}, s32[8,16,128]{2,1,0:T(8,128)}, u32[]{:S(2)}) copy-start(s32[8,16,128]{2,1,0:T(8,128)} %param.16) | copy-start | bytes 196612
  10.9 20.0 %collective-permute-start.1 = (f32[192,128]{1,0:T(8,128)S(1)}, f32[192,128]{1,0:T(8,128)S(1)}, u32[]{:S(2)}, u32[]{:S(2)}) collective-permute-start(f32[192,128]{1,0:T(8,128)S(1)} %get-tuple-element.9.own_ref), channel_id=1, source_target_pairs={{8,0},{16,8},{24,16},{32,24},{40,32},{48,40},{56,48},{64,56},{72,6... | collective-permute-start | bytes 294920 | tf_op jit(solution)/shard_map/ppermute | solution.py:394
  13.5 17.5 %collective-permute-start = (f32[192,128]{1,0:T(8,128)S(1)}, f32[192,128]{1,0:T(8,128)S(1)}, u32[]{:S(2)}, u32[]{:S(2)}) collective-permute-start(f32[192,128]{1,0:T(8,128)S(1)} %get-tuple-element.9.own_ref), channel_id=1, source_target_pairs={{0,8},{8,16},{16,24},{24,32},{32,40},{40,48},{48,56},{56,64},{64,7... | collective-permute-start | bytes 294920 | tf_op jit(solution)/shard_map/ppermute | solution.py:394
  15.4 8.3 %collective-permute-start.2 = (f32[24,128]{1,0:T(8,128)S(1)}, f32[24,128]{1,0:T(8,128)S(1)}, u32[]{:S(2)}, u32[]{:S(2)}) collective-permute-start(f32[24,128]{1,0:T(8,128)S(1)} %get-tuple-element.10), channel_id=1, source_target_pairs={{0,16},{8,24},{16,32},{24,40},{32,48},{40,56},{48,64},{56,72},{64,... | collective-permute-start | bytes 36872 | tf_op jit(solution)/shard_map/ppermute | solution.py:394
  21.7 9.2 %collective-permute-start.3 = (f32[24,128]{1,0:T(8,128)S(1)}, f32[24,128]{1,0:T(8,128)S(1)}, u32[]{:S(2)}, u32[]{:S(2)}) collective-permute-start(f32[24,128]{1,0:T(8,128)S(1)} %get-tuple-element.11), channel_id=1, source_target_pairs={{16,0},{24,8},{32,16},{40,24},{48,32},{56,40},{64,48},{72,56},{80,... | collective-permute-start | bytes 36872 | tf_op jit(solution)/shard_map/ppermute | solution.py:394
  31.0 7.3 %collective-permute-start.5 = (f32[216,128]{1,0:T(8,128)S(1)}, f32[216,128]{1,0:T(8,128)S(1)}, u32[]{:S(2)}, u32[]{:S(2)}) collective-permute-start(f32[216,128]{1,0:T(8,128)S(1)} %get-tuple-element.12.left_ref), channel_id=1, source_target_pairs={{1,0},{2,1},{3,2},{4,3},{5,4},{6,5},{7,6},{9,8},{10,9},{11,10},{12... | collective-permute-start | bytes 331784 | tf_op jit(solution)/shard_map/ppermute | solution.py:394
  35.8 8.8 %collective-permute-start.4 = (f32[216,128]{1,0:T(8,128)S(1)}, f32[216,128]{1,0:T(8,128)S(1)}, u32[]{:S(2)}, u32[]{:S(2)}) collective-permute-start(f32[216,128]{1,0:T(8,128)S(1)} %get-tuple-element.13.right_ref), channel_id=1, source_target_pairs={{0,1},{1,2},{2,3},{3,4},{4,5},{5,6},{6,7},{8,9},{9,10},{10,11},{11... | collective-permute-start | bytes 331784 | tf_op jit(solution)/shard_map/ppermute | solution.py:394
  44.6 1.1 %copy-start.2 = (bf16[3,384,256]{2,1,0:T(8,128)(2,1)S(1)}, bf16[3,384,256]{2,1,0:T(8,128)(2,1)}, u32[]{:S(2)}) copy-start(bf16[3,384,256]{2,1,0:T(8,128)(2,1)} %constant.20.clone.x_lower_ref) | copy-start | bytes 1769476
  45.6 1.1 %copy-start.3 = (bf16[3,384,256]{2,1,0:T(8,128)(2,1)S(1)}, bf16[3,384,256]{2,1,0:T(8,128)(2,1)}, u32[]{:S(2)}) copy-start(bf16[3,384,256]{2,1,0:T(8,128)(2,1)} %constant.19.clone.x_upper_ref) | copy-start | bytes 1769476

commit v2 on v1

--- a/solution.py
+++ b/solution.py
@@ -20,7 +20,12 @@
 RADII = (RIM // 4, RIM // 2, RIM)
 VESSEL_GAIN = 4.0
 TUBE_FLOOR = 0.01
-VMEM_LIMIT = 40 * 1024 * 1024
+PATCH = SPAN_Z * CX + 2 * 16
+CHIP_ROWS = 2 * CZ + 2
+EDGE = 168
+SEND_ROWS = CHIP_ROWS // 2
+VMEM_LIMIT = 24 * 1024 * 1024
+DECODER_VMEM_LIMIT = 63 * 1024 * 1024
 
 
 def window(size):
@@ -123,26 +128,44 @@
 
 def column_of(row_ref):
     eye = iota((CHANNELS, CHANNELS), 0) == iota((CHANNELS, CHANNELS), 1)
-    return jnp.sum(jnp.where(eye, row_ref[...], 0.0), axis=1, keepdims=True)
+    row = row_ref[...].astype(jnp.float32)
+    return jnp.sum(jnp.where(eye, row, 0.0), axis=1, keepdims=True)
 
 
 def decoder_kernel(
+    features_hbm,
+    weight1_hbm,
+    bias1_hbm,
+    weight2_hbm,
+    bias2_hbm,
+    head_hbm,
+    patch_ref,
     features_ref,
     weight1_ref,
     bias1_ref,
     weight2_ref,
     bias2_ref,
     head_ref,
-    patch_ref,
-    low_ref,
-    high_ref,
     first_ref,
     second_ref,
     wide1_ref,
     wide2_ref,
+    arrived,
 ):
-    expand_weight(weight1_ref, wide1_ref)
-    expand_weight(weight2_ref, wide2_ref)
+    routes = (
+        (weight1_hbm, weight1_ref),
+        (weight2_hbm, weight2_ref),
+        (bias1_hbm, bias1_ref),
+        (bias2_hbm, bias2_ref),
+        (head_hbm, head_ref),
+        (features_hbm, features_ref),
+    )
+    copies = [
+        pltpu.make_async_copy(source, target, arrived.at[k])
+        for k, (source, target) in enumerate(routes)
+    ]
+    for copy in copies:
+        copy.start()
     for ref in (first_ref, second_ref):
         ref[0:SLOT, 0:YC] = jnp.zeros((SLOT, YC), jnp.bfloat16)
         ref[(HALF + 1) * SLOT :, YC:] = jnp.zeros((SLOT, YC), jnp.bfloat16)
@@ -150,6 +173,12 @@
             ref[slot * SLOT + 3 * ROWS : (slot + 1) * SLOT, :] = jnp.zeros(
                 (SLOT - 3 * ROWS, 2 * YC), jnp.bfloat16
             )
+    copies[0].wait()
+    expand_weight(weight1_ref, wide1_ref)
+    copies[1].wait()
+    expand_weight(weight2_ref, wide2_ref)
+    for copy in copies[2:]:
+        copy.wait()
     for x in range(SPAN_X):
         column = features_ref[:, x].reshape(ROWS, YC).astype(jnp.float32)
         three = [v.astype(jnp.bfloat16) for v in y_neighbours(column)]
@@ -192,8 +221,6 @@
     place = iota((16, YC), 0).astype(jnp.float32)
     centred = (place - (SPAN_Z - 1) / 2.0) / (SPAN_Z / 4.0)
     weight_z = jnp.exp(-0.5 * centred * centred)
-    low_ref[16:24] = jnp.zeros((8, YC), jnp.float32)
-    high_ref[16:24] = jnp.zeros((8, YC), jnp.float32)
     for step in range(HALF):
         hidden = layer(wide2_ref, second_ref, bias2, step).astype(jnp.bfloat16)
         logits = jnp.dot(head, hidden, preferred_element_type=jnp.float32)
@@ -203,47 +230,84 @@
             if x == 0 or x == SPAN_X - 1:
                 side = 0 if x == 0 else 1
                 patch_ref[160 + side * 16 : 176 + side * 16, :] = weighted
-                row = 16 + side
             else:
                 patch_ref[pl.ds(x - 1, SPAN_Z, stride=CX), :] = weighted[:SPAN_Z]
-                row = x - 1
-            low_ref[row : row + 1, :] = weighted[0:1]
-            high_ref[row : row + 1, :] = weighted[SPAN_Z - 1 : SPAN_Z]
-
-
-def slab_kernel(below_ref, own_ref, above_ref, far_below_ref, far_above_ref, left_ref, right_ref):
-    refs = (below_ref, own_ref, above_ref)
-    row = iota((CZ, YC), 0)
-    for block in range(3):
-        ref = refs[block]
-        for i in range(CZ):
-            value = ref[(i + 1) * CX : (i + 2) * CX, :]
-            if i == 0:
-                if block == 0:
-                    value = value + far_below_ref[0:CX]
-                else:
-                    value = value + refs[block - 1][9 * CX : 10 * CX, :]
-            if i == CZ - 1:
-                if block == 2:
-                    value = value + far_above_ref[0:CX]
-                else:
-                    value = value + refs[block + 1][0:CX, :]
-            z = block * CZ + i
-            left_ref[z * 8 : (z + 1) * 8, :] = value[:8]
-            right_ref[z * 8 : (z + 1) * 8, :] = value[8:]
-        for side, out_ref in enumerate((left_ref, right_ref)):
-            base = 160 + side * 16
-            value = ref[base + 1 : base + 9, :]
-            if block == 0:
-                lower = far_below_ref[16 + side : 17 + side]
+
+
+def chip_row(pair_ref, r):
+    low, high = r + 1, r - CZ + 1
+    value = None
+    for patch, index in ((0, low), (1, high)):
+        if 0 <= index < SPAN_Z:
+            base = patch * PATCH + index * CX
+            part = pair_ref[base : base + CX, :]
+            value = part if value is None else value + part
+    return value
+
+
+def chip_margin(pair_ref, side, r):
+    low, high = r + 1, r - CZ + 1
+    value = None
+    for patch, index in ((0, low), (1, high)):
+        if 0 <= index < SPAN_Z:
+            base = patch * PATCH + SPAN_Z * CX + side * 16 + index
+            part = pair_ref[base : base + 1, :]
+            value = part if value is None else value + part
+    return value
+
+
+def edge_kernel(place_ref, pair_ref, edge_ref):
+    to_right = place_ref[4] == 1
+    for n in range(CHIP_ROWS):
+        value = chip_row(pair_ref, n - 1)
+        edge_ref[n * 8 : (n + 1) * 8, :] = jnp.where(to_right, value[8:], value[:8])
+        left, right = (chip_margin(pair_ref, side, n - 1) for side in range(2))
+        edge_ref[CHIP_ROWS * 8 + n : CHIP_ROWS * 8 + n + 1, :] = jnp.where(to_right, right, left)
+    edge_ref[CHIP_ROWS * 9 :, :] = jnp.zeros((EDGE - CHIP_ROWS * 9, YC), jnp.float32)
+
+
+def chip_kernel(place_ref, pair_ref, edges_ref, chip_ref, send_ref):
+    at_x, count_x, odd_x = place_ref[2], place_ref[3], place_ref[5]
+    from_left = (1 - odd_x) * (2 * EDGE)
+    from_right = odd_x * (2 * EDGE) + EDGE
+    sub = iota((8, YC), 0)
+    has_left = jnp.where(at_x > 0, 1.0, 0.0)
+    has_right = jnp.where(at_x < count_x - 1, 1.0, 0.0)
+    upper_core = place_ref[6] == 1
+
+    def part(start, offset, count):
+        return edges_ref[pl.ds(pl.multiple_of(start, 8) + offset, count), :]
+
+    left_margins = [part(from_left, CHIP_ROWS * 8 + 8 * n, 8) * has_left for n in range(3)]
+    right_margins = [part(from_right, CHIP_ROWS * 8 + 8 * n, 8) * has_right for n in range(3)]
+    for n in range(CHIP_ROWS):
+        own = chip_row(pair_ref, n - 1)
+        first_margin, last_margin = (chip_margin(pair_ref, side, n - 1) for side in range(2))
+        block, at = divmod(n, 8)
+        left_margin = left_margins[block][at : at + 1]
+        right_margin = right_margins[block][at : at + 1]
+        sums = (
+            part(from_left, n * 8, 8) * has_left + jnp.where(sub == 7, first_margin, 0.0),
+            own[:8] + jnp.where(sub == 0, left_margin, 0.0),
+            own[8:] + jnp.where(sub == 7, right_margin, 0.0),
+            part(from_right, n * 8, 8) * has_right + jnp.where(sub == 0, last_margin, 0.0),
+        )
+        for k in range(4):
+            at = n * 32 + k * 8
+            chip_ref[at : at + 8, :] = sums[k]
+            low = k * 8 + n * 32
+            high = k * 8 + (n - SEND_ROWS) * 32
+            if n < SEND_ROWS:
+
+                @pl.when(jnp.logical_not(upper_core))
+                def _(value=sums[k], low=low):
+                    send_ref[low : low + 8, :] = value
+
             else:
-                lower = refs[block - 1][base + 9 : base + 10, :]
-            if block == 2:
-                upper = far_above_ref[16 + side : 17 + side]
-            else:
-                upper = refs[block + 1][base : base + 1, :]
-            value = value + jnp.where(row == 0, lower, 0.0) + jnp.where(row == CZ - 1, upper, 0.0)
-            out_ref[192 + block * 8 : 200 + block * 8, :] = value
+
+                @pl.when(upper_core)
+                def _(value=sums[k], high=high):
+                    send_ref[high : high + 8, :] = value
 
 
 def two_terms(values):
@@ -254,10 +318,9 @@
 
 def vessel_kernel(
     place_ref,
-    left_ref,
-    right_ref,
-    from_left_ref,
-    from_right_ref,
+    chip_ref,
+    slabs_ref,
+    rows_ref,
     tissue_ref,
     x_upper_ref,
     x_lower_ref,
@@ -267,6 +330,39 @@
     extended_ref,
     along_z_ref,
 ):
+    upper_core = place_ref[6] == 1
+
+    below = jnp.where(place_ref[0] - place_ref[6] > 0, 1.0, 0.0)
+    above = jnp.where(place_ref[0] - place_ref[6] < place_ref[1] - 2, 1.0, 0.0)
+
+    @pl.when(jnp.logical_not(upper_core))
+    def _():
+        for z in range(3 * CZ):
+            value = None
+            if z >= RIM - 1:
+                n = z - RIM + 1
+                value = chip_ref[n * 32 : (n + 1) * 32, :]
+            if z < SEND_ROWS:
+                part = slabs_ref[z * 32 : (z + 1) * 32, :] * below
+                value = part if value is None else value + part
+            if z == 3 * CZ - 1:
+                value = value + rows_ref[32:64, :] * above
+            extended_ref[z * 32 : (z + 1) * 32, :] = value
+
+    @pl.when(upper_core)
+    def _():
+        for z in range(3 * CZ):
+            value = None
+            if z + 1 < CHIP_ROWS:
+                value = chip_ref[(z + 1) * 32 : (z + 2) * 32, :]
+            if z >= 3 * CZ - SEND_ROWS:
+                n = SEND_ROWS + z - (3 * CZ - SEND_ROWS)
+                part = slabs_ref[n * 32 : (n + 1) * 32, :] * above
+                value = part if value is None else value + part
+            if z == 0:
+                value = value + rows_ref[0:32, :] * below
+            extended_ref[z * 32 : (z + 1) * 32, :] = value
+
     at_z, count_z, at_x, count_x = (place_ref[k] for k in range(4))
     sub = iota((8, YC), 0)
 
@@ -300,16 +396,9 @@
             scale = jnp.where(lower_there[block], float(1.0 / (plain + wz_last)), scale)
         if i == CZ - 1:
             scale = jnp.where(upper_there[block], float(1.0 / (plain + wz_first)), scale)
-        rows = slice(z * 8, (z + 1) * 8)
-        edge = slice(192 + z, 193 + z)
-        sums = (
-            from_left_ref[rows, :] + jnp.where(sub == 7, left_ref[edge, :], 0.0),
-            left_ref[rows, :] + jnp.where(sub == 0, from_left_ref[edge, :], 0.0),
-            right_ref[rows, :] + jnp.where(sub == 7, from_right_ref[edge, :], 0.0),
-            from_right_ref[rows, :] + jnp.where(sub == 0, right_ref[edge, :], 0.0),
-        )
         for k in range(4):
-            value = 1.0 / (1.0 + jnp.exp(-(sums[k] * (inverse[k] * scale))))
+            blended = extended_ref[z * 32 + k * 8 : z * 32 + k * 8 + 8, :]
+            value = 1.0 / (1.0 + jnp.exp(-(blended * (inverse[k] * scale))))
             if block == 1 and k in (1, 2):
                 at = i * CX + (k - 1) * 8
                 probability_ref[at : at + 8, :] = value
@@ -388,37 +477,75 @@
     vessel_ref[...] = VESSEL_GAIN * tissue_ref[...].astype(jnp.float32) * total
 
 
-def from_behind(block, axis, distance):
-    devices = range(lax.axis_size(axis))
-    route = [(i - distance, i) for i in devices if i - distance in devices]
-    return lax.ppermute(block, axis, route)
-
-
-def whole(count):
-    return [pl.BlockSpec(memory_space=pltpu.VMEM)] * count
+def pairs_of(kind, count_z, count_x):
+    def flat(z, x):
+        return (z % count_z) * count_x + x % count_x
+
+    if kind == "x":
+        return [
+            [flat(z, x), flat(z, x + 1)]
+            for z in range(count_z)
+            for x in range(z % 2, count_x + z % 2, 2)
+        ]
+    first = 0 if kind == "chip" else 1
+    return [
+        [flat(z, x), flat(z + 1, x)]
+        for z in range(first, count_z + first, 2)
+        for x in range(count_x)
+    ]
+
+
+def swap(block, kind):
+    groups = pairs_of(kind, lax.axis_size("gz"), lax.axis_size("xy"))
+    return lax.all_gather(block, ("gz", "xy"), axis_index_groups=groups, tiled=True)
+
+
+def whole(count, space=pltpu.VMEM):
+    return [pl.BlockSpec(memory_space=space)] * count
+
+
+def shape_of(*dims):
+    return jax.ShapeDtypeStruct(dims, jnp.float32)
 
 
 def on_device(
     patch_features, conv1_weight, conv1_bias, conv2_weight, conv2_bias, head_weight, tissue_mask
 ):
-    f32 = jnp.float32
+    f32, bf16 = jnp.float32, jnp.bfloat16
     params = pltpu.CompilerParams(vmem_limit_bytes=VMEM_LIMIT)
-    patch, low, high = pl.pallas_call(
+    at_z, at_x = lax.axis_index("gz"), lax.axis_index("xy")
+    place = jnp.stack(
+        [
+            at_z,
+            jnp.int32(lax.axis_size("gz")),
+            at_x,
+            jnp.int32(lax.axis_size("xy")),
+            1 - ((at_z + at_x) & 1),
+            at_x & 1,
+            at_z & 1,
+        ]
+    ).astype(jnp.int32)
+    weight_shape = (3, 3, 3, CHANNELS, CHANNELS)
+    slots = ((HALF + 2) * SLOT, 2 * YC)
+    patch = pl.pallas_call(
         decoder_kernel,
-        out_shape=(
-            jax.ShapeDtypeStruct((192, YC), f32),
-            jax.ShapeDtypeStruct((24, YC), f32),
-            jax.ShapeDtypeStruct((24, YC), f32),
-        ),
-        in_specs=whole(6),
-        out_specs=tuple(whole(3)),
+        out_shape=shape_of(PATCH, YC),
+        in_specs=whole(6, pltpu.HBM),
+        out_specs=whole(1)[0],
         scratch_shapes=[
-            pltpu.VMEM(((HALF + 2) * SLOT, 2 * YC), jnp.bfloat16),
-            pltpu.VMEM(((HALF + 2) * SLOT, 2 * YC), jnp.bfloat16),
-            pltpu.VMEM((ROWS, 3 * SLOT), jnp.bfloat16),
-            pltpu.VMEM((ROWS, 3 * SLOT), jnp.bfloat16),
+            pltpu.VMEM((SPAN_Z, SPAN_X, CHANNELS, YC), bf16),
+            pltpu.VMEM(weight_shape, bf16),
+            pltpu.VMEM((1, CHANNELS), f32),
+            pltpu.VMEM(weight_shape, bf16),
+            pltpu.VMEM((1, CHANNELS), f32),
+            pltpu.VMEM((1, CHANNELS), bf16),
+            pltpu.VMEM(slots, bf16),
+            pltpu.VMEM(slots, bf16),
+            pltpu.VMEM((ROWS, 3 * SLOT), bf16),
+            pltpu.VMEM((ROWS, 3 * SLOT), bf16),
+            pltpu.SemaphoreType.DMA((6,)),
         ],
-        compiler_params=params,
+        compiler_params=pltpu.CompilerParams(vmem_limit_bytes=DECODER_VMEM_LIMIT),
         name="decoder",
     )(
         patch_features.transpose(1, 2, 0, 3),
@@ -426,54 +553,48 @@
         conv1_bias.reshape(1, CHANNELS),
         conv2_weight.transpose(2, 3, 4, 0, 1),
         conv2_bias.reshape(1, CHANNELS),
-        head_weight.astype(f32).reshape(1, CHANNELS),
+        head_weight.reshape(1, CHANNELS),
     )
-    below = from_behind(patch, "gz", 1)
-    above = from_behind(patch, "gz", -1)
-    far_below = from_behind(high, "gz", 2)
-    far_above = from_behind(low, "gz", -2)
-    left, right = pl.pallas_call(
-        slab_kernel,
-        out_shape=(
-            jax.ShapeDtypeStruct((216, YC), f32),
-            jax.ShapeDtypeStruct((216, YC), f32),
-        ),
-        in_specs=whole(5),
+    smem = pl.BlockSpec(memory_space=pltpu.SMEM)
+    pair = swap(patch, "chip")
+    edge = pl.pallas_call(
+        edge_kernel,
+        out_shape=shape_of(EDGE, YC),
+        in_specs=[smem] + whole(1),
+        out_specs=whole(1)[0],
+        compiler_params=params,
+        name="edge",
+    )(place, pair)
+    edges = swap(swap(edge, "x"), "chip")
+    chip, send = pl.pallas_call(
+        chip_kernel,
+        out_shape=(shape_of(CHIP_ROWS * 32, YC), shape_of(SEND_ROWS * 32, YC)),
+        in_specs=[smem] + whole(2),
         out_specs=tuple(whole(2)),
         compiler_params=params,
-        name="slab",
-    )(below, patch, above, far_below, far_above)
-    from_left = from_behind(right, "xy", 1)
-    from_right = from_behind(left, "xy", -1)
-    place = jnp.stack(
-        [
-            lax.axis_index("gz"),
-            jnp.int32(lax.axis_size("gz")),
-            lax.axis_index("xy"),
-            jnp.int32(lax.axis_size("xy")),
-        ]
-    ).astype(jnp.int32)
+        name="chip",
+    )(place, pair, edges)
+    slabs = swap(send, "slab")
+    upper_core = at_z & 1
+    row_at = jnp.where(upper_core == 1, SEND_ROWS * 32, (SEND_ROWS - 1) * 32)
+    rows = swap(lax.dynamic_slice(slabs, (row_at, 0), (32, YC)), "chip")
     x_upper, x_lower, y_all = filter_constants()
     probability, vesselness = pl.pallas_call(
         vessel_kernel,
-        out_shape=(
-            jax.ShapeDtypeStruct((CZ * CX, YC), f32),
-            jax.ShapeDtypeStruct((CZ * CX, YC), f32),
-        ),
-        in_specs=[pl.BlockSpec(memory_space=pltpu.SMEM)] + whole(8),
+        out_shape=(shape_of(CZ * CX, YC), shape_of(CZ * CX, YC)),
+        in_specs=[smem] + whole(7),
         out_specs=tuple(whole(2)),
         scratch_shapes=[
             pltpu.VMEM((3 * CZ * 32, YC), f32),
-            pltpu.VMEM((9 * 256, 2 * YC), jnp.bfloat16),
+            pltpu.VMEM((9 * 256, 2 * YC), bf16),
         ],
         compiler_params=params,
         name="vessel",
     )(
         place,
-        left,
-        right,
-        from_left,
-        from_right,
+        chip,
+        slabs,
+        rows,
         tissue_mask.reshape(CZ * CX, YC),
         jnp.asarray(x_upper),
         jnp.asarray(x_lower),

time: 50.7 us -> 41.9 us (0.83)
  the two profiles are of different devices: /device:TPU:120 before, /device:TPU:1 now
where the time goes in v2:
time: 41.9 us; the launch traced here: 41.7 us
  blocking collectives  28.8 us (69%)
  Pallas kernels  12.1 us (29%)
  between operations  0.7 us (2%)
    all_gather x5, blocking collectives, swap(): lax.all_gather(block, ('gz', 'xy'), axis_index_groups=groups, tiled=True)  28.8 us
    pallas_call x1, Pallas kernels, on_device(): pl.pallas_call(decoder_kernel, out_shape=shape_of(PATCH, YC), in_specs=wh...  7.25 us
    pallas_call x1, Pallas kernels, on_device(): pl.pallas_call(vessel_kernel, out_shape=(shape_of(CZ * CX, YC), shape_of(...  3.56 us

profile of v2, /device:TPU:1, one launch (start us, length us, event | category | flops | bytes accessed | tf_op | source)
XLA Modules:
  0.0 41.7 jit_solution(547816091772160993)
XLA Ops:
  0.6 0.1 stack.23.place_ref
  0.7 0.0 copy-start.3
  0.7 7.3 %decoder.1 = f32[192,128]{1,0:T(8,128)} custom-call(bf16[10,18,16,128]{3,2,1,0:T(8,128)(2,1)} %bitcast.15, bf16[3,3,3,16,16]{4,3,2,1,0:T(8,128)(2,1)} %bitcast.16, f32[1,16]{1,0:T(1,128)} %bitcast.18, bf16[3,3,3,16,16]{4,3,2,1,0:T(8,128)(2,1)} %bitcast.17, f32[1,16]{1,0:T(1,128)} %bitcast.19, bf16[1,16]{1,0:T(2,128)(2,1)} %bitcast.20), custom_call_target="tpu_custom_call" | custom-call | tf_op jit(solution)/shard_map/decoder/pallas_call | solution.py:530
  8.0 0.0 copy-start
  8.0 0.0 copy-start.1
  8.0 0.0 copy-start.2
  8.0 8.8 %all_gather.15.pair_ref = f32[384,128]{1,0:T(8,128)S(1)} all-gather(f32[192,128]{1,0:T(8,128)} %decoder.1), channel_id=1, replica_groups={{0,8},{1,9},{2,10},{3,11},{4,12},{5,13},{6,14},{7,15},{16,24},{17,25},{..., dimensions={0}, use_global_device_ids=true | all-gather | bytes 294912 | tf_op jit(solution)/shard_map/all_gather | solution.py:500
  16.8 0.6 %edge.1 = f32[168,128]{1,0:T(8,128)S(1)} custom-call(s32[7]{0:T(128)S(1)} %stack.23.place_ref, f32[384,128]{1,0:T(8,128)S(1)} %all_gather.15.pair_ref), custom_call_target="tpu_custom_call" | custom-call | tf_op jit(solution)/shard_map/edge/pallas_call | solution.py:560
  17.4 6.1 %all_gather.16 = f32[336,128]{1,0:T(8,128)S(1)} all-gather(f32[168,128]{1,0:T(8,128)S(1)} %edge.1), channel_id=1, replica_groups={{0,1},{2,3},{4,5},{6,7},{9,10},{11,12},{13,14},{15,8},{16,17},{18,19},{..., dimensions={0}, use_global_device_ids=true | all-gather | bytes 258048 | tf_op jit(solution)/shard_map/all_gather | solution.py:500
  23.5 2.0 %all_gather.17.edges_ref = f32[672,128]{1,0:T(8,128)S(1)} all-gather(f32[336,128]{1,0:T(8,128)S(1)} %all_gather.16), channel_id=1, replica_groups={{0,8},{1,9},{2,10},{3,11},{4,12},{5,13},{6,14},{7,15},{16,24},{17,25},{..., dimensions={0}, use_global_device_ids=true | all-gather | bytes 516096 | tf_op jit(solution)/shard_map/all_gather | solution.py:500
  25.6 0.8 %chip.1 = (f32[576,128]{1,0:T(8,128)S(1)}, f32[288,128]{1,0:T(8,128)S(1)}) custom-call(s32[7]{0:T(128)S(1)} %stack.23.place_ref, f32[384,128]{1,0:T(8,128)S(1)} %all_gather.15.pair_ref, f32[672,128]{1,0:T(8,128)S(1)} %all_gather.17.edges_ref), custom_call_target="tpu_custom_call" | custom-call | tf_op jit(solution)/shard_map/chip/pallas_call | solution.py:569
  26.3 6.7 %all_gather.18.slabs_ref = f32[576,128]{1,0:T(8,128)S(1)} all-gather(f32[288,128]{1,0:T(8,128)S(1)} %get-tuple-element.7), channel_id=1, replica_groups={{8,16},{9,17},{10,18},{11,19},{12,20},{13,21},{14,22},{15,23},{24,32},{..., dimensions={0}, use_global_device_ids=true | all-gather | bytes 442368 | tf_op jit(solution)/shard_map/all_gather | solution.py:500
  33.1 5.1 %all_gather.19.rows_ref = f32[64,128]{1,0:T(8,128)S(1)} all-gather(f32[32,128]{1,0:T(8,128)S(1)} %constant_dynamic-slice_fusion), channel_id=1, replica_groups={{0,8},{1,9},{2,10},{3,11},{4,12},{5,13},{6,14},{7,15},{16,24},{17,25},{..., dimensions={0}, use_global_device_ids=true | all-gather | bytes 49152 | tf_op jit(solution)/shard_map/all_gather | solution.py:500
  38.2 0.0 copy-done.3
  38.2 0.0 copy-done
  38.2 0.0 copy-done.1
  38.2 0.0 copy-done.2
  38.2 3.6 %vessel.1 = (f32[128,128]{1,0:T(8,128)}, f32[128,128]{1,0:T(8,128)}) custom-call(s32[7]{0:T(128)S(1)} %stack.23.place_ref, f32[576,128]{1,0:T(8,128)S(1)} %get-tuple-element.6.chip_ref, f32[576,128]{1,0:T(8,128)S(1)} %all_gather.18.slabs_ref, f32[64,128]{1,0:T(8,128)S(1)} %all_gather.19.rows_ref, s32[128,128]{1,0:T(8,128)S(1)} %bitcast.14, ...), custom_call_target="tpu_custom_call" | custom-call | tf_op jit(solution)/shard_map/vessel/pallas_call | solution.py:582
  (1 shorter events, 0.0 us)
Async XLA Ops:
  0.7 37.4 %copy-start.3 = (s32[8,16,128]{2,1,0:T(8,128)S(1)}, s32[8,16,128]{2,1,0:T(8,128)}, u32[]{:S(2)}) copy-start(s32[8,16,128]{2,1,0:T(8,128)} %param.16) | copy-start | bytes 196612
  8.0 30.2 %copy-start = (bf16[9,256,256]{2,1,0:T(8,128)(2,1)S(1)}, bf16[9,256,256]{2,1,0:T(8,128)(2,1)}, u32[]{:S(2)}) copy-start(bf16[9,256,256]{2,1,0:T(8,128)(2,1)} %constant.31.clone.y_ref) | copy-start | bytes 3538948
  8.0 30.2 %copy-start.1 = (bf16[3,384,256]{2,1,0:T(8,128)(2,1)S(1)}, bf16[3,384,256]{2,1,0:T(8,128)(2,1)}, u32[]{:S(2)}) copy-start(bf16[3,384,256]{2,1,0:T(8,128)(2,1)} %constant.30.clone.x_lower_ref) | copy-start | bytes 1769476
  8.0 30.2 %copy-start.2 = (bf16[3,384,256]{2,1,0:T(8,128)(2,1)S(1)}, bf16[3,384,256]{2,1,0:T(8,128)(2,1)}, u32[]{:S(2)}) copy-start(bf16[3,384,256]{2,1,0:T(8,128)(2,1)} %constant.29.clone.x_upper_ref) | copy-start | bytes 1769476

commit v3 on v2

--- a/solution.py
+++ b/solution.py
@@ -150,6 +150,7 @@
     second_ref,
     wide1_ref,
     wide2_ref,
+    last_ref,
     arrived,
 ):
     routes = (
@@ -223,10 +224,13 @@
     weight_z = jnp.exp(-0.5 * centred * centred)
     for step in range(HALF):
         hidden = layer(wide2_ref, second_ref, bias2, step).astype(jnp.bfloat16)
-        logits = jnp.dot(head, hidden, preferred_element_type=jnp.float32)
+        last_ref[:, step * 2 * YC : (step + 1) * 2 * YC] = hidden
+    logits = jnp.dot(head, last_ref[...], preferred_element_type=jnp.float32)
+    for step in range(HALF):
         for half in range(2):
             x = step + half * HALF
-            weighted = logits[:, half * YC : (half + 1) * YC] * (weight_z * float(WINDOW_X[x]))
+            at = (step * 2 + half) * YC
+            weighted = logits[:, at : at + YC] * (weight_z * float(WINDOW_X[x]))
             if x == 0 or x == SPAN_X - 1:
                 side = 0 if x == 0 else 1
                 patch_ref[160 + side * 16 : 176 + side * 16, :] = weighted
@@ -256,8 +260,13 @@
     return value
 
 
-def edge_kernel(place_ref, pair_ref, edge_ref):
-    to_right = place_ref[4] == 1
+def position():
+    return lax.axis_index("gz"), lax.axis_size("gz"), lax.axis_index("xy"), lax.axis_size("xy")
+
+
+def edge_kernel(pair_ref, edge_ref):
+    at_z, _, at_x, _ = position()
+    to_right = ((at_z + at_x) & 1) == 0
     for n in range(CHIP_ROWS):
         value = chip_row(pair_ref, n - 1)
         edge_ref[n * 8 : (n + 1) * 8, :] = jnp.where(to_right, value[8:], value[:8])
@@ -266,14 +275,15 @@
     edge_ref[CHIP_ROWS * 9 :, :] = jnp.zeros((EDGE - CHIP_ROWS * 9, YC), jnp.float32)
 
 
-def chip_kernel(place_ref, pair_ref, edges_ref, chip_ref, send_ref):
-    at_x, count_x, odd_x = place_ref[2], place_ref[3], place_ref[5]
+def chip_kernel(pair_ref, edges_ref, chip_ref, send_ref):
+    at_z, _, at_x, count_x = position()
+    odd_x = at_x & 1
     from_left = (1 - odd_x) * (2 * EDGE)
     from_right = odd_x * (2 * EDGE) + EDGE
     sub = iota((8, YC), 0)
     has_left = jnp.where(at_x > 0, 1.0, 0.0)
     has_right = jnp.where(at_x < count_x - 1, 1.0, 0.0)
-    upper_core = place_ref[6] == 1
+    upper_core = (at_z & 1) == 1
 
     def part(start, offset, count):
         return edges_ref[pl.ds(pl.multiple_of(start, 8) + offset, count), :]
@@ -317,7 +327,6 @@
 
 
 def vessel_kernel(
-    place_ref,
     chip_ref,
     slabs_ref,
     rows_ref,
@@ -330,10 +339,10 @@
     extended_ref,
     along_z_ref,
 ):
-    upper_core = place_ref[6] == 1
-
-    below = jnp.where(place_ref[0] - place_ref[6] > 0, 1.0, 0.0)
-    above = jnp.where(place_ref[0] - place_ref[6] < place_ref[1] - 2, 1.0, 0.0)
+    at_z, count_z, at_x, count_x = position()
+    upper_core = (at_z & 1) == 1
+    below = jnp.where(at_z - (at_z & 1) > 0, 1.0, 0.0)
+    above = jnp.where(at_z - (at_z & 1) < count_z - 2, 1.0, 0.0)
 
     @pl.when(jnp.logical_not(upper_core))
     def _():
@@ -363,7 +372,6 @@
                 value = value + rows_ref[0:32, :] * below
             extended_ref[z * 32 : (z + 1) * 32, :] = value
 
-    at_z, count_z, at_x, count_x = (place_ref[k] for k in range(4))
     sub = iota((8, YC), 0)
 
     def inverse_x(first, edge, edge_row, present):
@@ -481,18 +489,24 @@
     def flat(z, x):
         return (z % count_z) * count_x + x % count_x
 
-    if kind == "x":
+    if kind == "chip":
         return [
-            [flat(z, x), flat(z, x + 1)]
-            for z in range(count_z)
-            for x in range(z % 2, count_x + z % 2, 2)
+            [flat(z, x), flat(z + 1, x)] for z in range(0, count_z, 2) for x in range(count_x)
         ]
-    first = 0 if kind == "chip" else 1
-    return [
-        [flat(z, x), flat(z + 1, x)]
-        for z in range(first, count_z + first, 2)
-        for x in range(count_x)
+    if kind == "slab":
+        pairs = [
+            [flat(z, x), flat(z + 1, x)] for z in range(1, count_z - 1, 2) for x in range(count_x)
+        ]
+        return pairs + [
+            [flat(z, x), flat(z, x + 1)] for z in (0, count_z - 1) for x in range(0, count_x, 2)
+        ]
+    pairs = [
+        [flat(z, x), flat(z, x + 1)] for z in range(count_z) for x in range(z % 2, count_x - 1, 2)
     ]
+    if count_z % 8 == 0:
+        idle = [(z, z + 4) for z in range(1, count_z, 2) if z % 8 < 4]
+        return pairs + [[flat(z, x), flat(up, x)] for z, up in idle for x in (0, count_x - 1)]
+    return pairs + [[flat(z, count_x - 1), flat(z, 0)] for z in range(1, count_z, 2)]
 
 
 def swap(block, kind):
@@ -508,26 +522,11 @@
     return jax.ShapeDtypeStruct(dims, jnp.float32)
 
 
-def on_device(
-    patch_features, conv1_weight, conv1_bias, conv2_weight, conv2_bias, head_weight, tissue_mask
-):
+def decode(patch_features, conv1_weight, conv1_bias, conv2_weight, conv2_bias, head_weight):
     f32, bf16 = jnp.float32, jnp.bfloat16
-    params = pltpu.CompilerParams(vmem_limit_bytes=VMEM_LIMIT)
-    at_z, at_x = lax.axis_index("gz"), lax.axis_index("xy")
-    place = jnp.stack(
-        [
-            at_z,
-            jnp.int32(lax.axis_size("gz")),
-            at_x,
-            jnp.int32(lax.axis_size("xy")),
-            1 - ((at_z + at_x) & 1),
-            at_x & 1,
-            at_z & 1,
-        ]
-    ).astype(jnp.int32)
     weight_shape = (3, 3, 3, CHANNELS, CHANNELS)
     slots = ((HALF + 2) * SLOT, 2 * YC)
-    patch = pl.pallas_call(
+    return pl.pallas_call(
         decoder_kernel,
         out_shape=shape_of(PATCH, YC),
         in_specs=whole(6, pltpu.HBM),
@@ -543,6 +542,7 @@
             pltpu.VMEM(slots, bf16),
             pltpu.VMEM((ROWS, 3 * SLOT), bf16),
             pltpu.VMEM((ROWS, 3 * SLOT), bf16),
+            pltpu.VMEM((ROWS, SPAN_X * YC), bf16),
             pltpu.SemaphoreType.DMA((6,)),
         ],
         compiler_params=pltpu.CompilerParams(vmem_limit_bytes=DECODER_VMEM_LIMIT),
@@ -555,34 +555,43 @@
         conv2_bias.reshape(1, CHANNELS),
         head_weight.reshape(1, CHANNELS),
     )
-    smem = pl.BlockSpec(memory_space=pltpu.SMEM)
+
+
+def on_device(
+    patch_features, conv1_weight, conv1_bias, conv2_weight, conv2_bias, head_weight, tissue_mask
+):
+    f32, bf16 = jnp.float32, jnp.bfloat16
+    params = pltpu.CompilerParams(vmem_limit_bytes=VMEM_LIMIT)
+    patch = decode(
+        patch_features, conv1_weight, conv1_bias, conv2_weight, conv2_bias, head_weight
+    )
     pair = swap(patch, "chip")
     edge = pl.pallas_call(
         edge_kernel,
         out_shape=shape_of(EDGE, YC),
-        in_specs=[smem] + whole(1),
+        in_specs=whole(1),
         out_specs=whole(1)[0],
         compiler_params=params,
         name="edge",
-    )(place, pair)
+    )(pair)
     edges = swap(swap(edge, "x"), "chip")
     chip, send = pl.pallas_call(
         chip_kernel,
         out_shape=(shape_of(CHIP_ROWS * 32, YC), shape_of(SEND_ROWS * 32, YC)),
-        in_specs=[smem] + whole(2),
+        in_specs=whole(2),
         out_specs=tuple(whole(2)),
         compiler_params=params,
         name="chip",
-    )(place, pair, edges)
+    )(pair, edges)
     slabs = swap(send, "slab")
-    upper_core = at_z & 1
+    upper_core = lax.axis_index("gz") & 1
     row_at = jnp.where(upper_core == 1, SEND_ROWS * 32, (SEND_ROWS - 1) * 32)
     rows = swap(lax.dynamic_slice(slabs, (row_at, 0), (32, YC)), "chip")
     x_upper, x_lower, y_all = filter_constants()
     probability, vesselness = pl.pallas_call(
         vessel_kernel,
         out_shape=(shape_of(CZ * CX, YC), shape_of(CZ * CX, YC)),
-        in_specs=[smem] + whole(7),
+        in_specs=whole(7),
         out_specs=tuple(whole(2)),
         scratch_shapes=[
             pltpu.VMEM((3 * CZ * 32, YC), f32),
@@ -591,7 +600,6 @@
         compiler_params=params,
         name="vessel",
     )(
-        place,
         chip,
         slabs,
         rows,

time: 41.9 us -> 34.2 us (0.82)
  blocking collectives: 28.8 us -> 24.6 us
  Pallas kernels: 12.1 us -> 8.77 us
    all_gather x5, blocking collectives: 28.8 us -> 24.6 us  [swap(): lax.all_gather(block, ('gz', 'xy'), axis_index_groups=groups, tiled=True)]
    pallas_call x2, Pallas kernels: 7.81 us -> 5.58 us  [the longest x1 5.56 us: decode(): pl.pallas_call(decoder_kernel, out_shape=shape_of(PATCH, YC), in_specs=wh...]
    pallas_call x1, Pallas kernels: 3.56 us -> 2.99 us  [on_device(): pl.pallas_call(vessel_kernel, out_shape=(shape_of(CZ * CX, YC), shape_of(...]
    pallas_call x1, Pallas kernels: 0.75 us -> 0.2 us  [on_device(): pl.pallas_call(chip_kernel, out_shape=(shape_of(CHIP_ROWS * 32, YC), shap...]
where the time goes in v3:
time: 34.2 us; the launch traced here: 34.1 us
  blocking collectives  24.6 us (72%)
  Pallas kernels  8.77 us (26%)
  between operations  0.7 us (2%)
    all_gather x5, blocking collectives, swap(): lax.all_gather(block, ('gz', 'xy'), axis_index_groups=groups, tiled=True)  24.6 us
    pallas_call x1, Pallas kernels, decode(): pl.pallas_call(decoder_kernel, out_shape=shape_of(PATCH, YC), in_specs=wh...  5.56 us
    pallas_call x1, Pallas kernels, on_device(): pl.pallas_call(vessel_kernel, out_shape=(shape_of(CZ * CX, YC), shape_of(...  2.99 us

profile of v3, /device:TPU:1, one launch (start us, length us, event | category | flops | bytes accessed | tf_op | source)
XLA Modules:
  0.0 34.1 jit_solution(13535392342691720917)
XLA Ops:
  0.6 5.6 %decoder.1 = f32[192,128]{1,0:T(8,128)} custom-call(bf16[10,18,16,128]{3,2,1,0:T(8,128)(2,1)} %bitcast.10, bf16[3,3,3,16,16]{4,3,2,1,0:T(8,128)(2,1)} %bitcast.11, f32[1,16]{1,0:T(1,128)} %bitcast.13, bf16[3,3,3,16,16]{4,3,2,1,0:T(8,128)(2,1)} %bitcast.12, f32[1,16]{1,0:T(1,128)} %bitcast.14, bf16[1,16]{1,0:T(2,128)(2,1)} %bitcast.15), custom_call_target="tpu_custom_call" | custom-call | tf_op jit(solution)/shard_map/decoder/pallas_call | solution.py:529
  6.2 0.0 copy-start
  6.2 0.0 copy-start.1
  6.2 0.0 copy-start.2
  6.2 0.0 copy-start.3
  6.2 8.8 %all_gather.15.pair_ref = f32[384,128]{1,0:T(8,128)S(1)} all-gather(f32[192,128]{1,0:T(8,128)} %decoder.1), channel_id=1, replica_groups={{0,8},{1,9},{2,10},{3,11},{4,12},{5,13},{6,14},{7,15},{16,24},{17,25},{..., dimensions={0}, use_global_device_ids=true | all-gather | bytes 294912 | tf_op jit(solution)/shard_map/all_gather | solution.py:514
  15.1 4.3 %all_gather.16 = f32[336,128]{1,0:T(8,128)S(1)} all-gather(f32[168,128]{1,0:T(8,128)S(1)} %edge.1), channel_id=1, replica_groups={{0,1},{2,3},{4,5},{6,7},{9,10},{11,12},{13,14},{16,17},{18,19},{20,21},..., dimensions={0}, use_global_device_ids=true | all-gather | bytes 258048 | tf_op jit(solution)/shard_map/all_gather | solution.py:514
  19.4 2.9 %all_gather.17.edges_ref = f32[672,128]{1,0:T(8,128)S(1)} all-gather(f32[336,128]{1,0:T(8,128)S(1)} %all_gather.16), channel_id=1, replica_groups={{0,8},{1,9},{2,10},{3,11},{4,12},{5,13},{6,14},{7,15},{16,24},{17,25},{..., dimensions={0}, use_global_device_ids=true | all-gather | bytes 516096 | tf_op jit(solution)/shard_map/all_gather | solution.py:514
  22.3 0.2 chip.1
  22.5 6.7 %all_gather.18.slabs_ref = f32[576,128]{1,0:T(8,128)S(1)} all-gather(f32[288,128]{1,0:T(8,128)S(1)} %get-tuple-element.7), channel_id=1, replica_groups={{8,16},{9,17},{10,18},{11,19},{12,20},{13,21},{14,22},{15,23},{24,32},{..., dimensions={0}, use_global_device_ids=true | all-gather | bytes 442368 | tf_op jit(solution)/shard_map/all_gather | solution.py:514
  29.2 1.8 %all_gather.19.rows_ref = f32[64,128]{1,0:T(8,128)S(1)} all-gather(f32[32,128]{1,0:T(8,128)S(1)} %constant_dynamic-slice_fusion), channel_id=1, replica_groups={{0,8},{1,9},{2,10},{3,11},{4,12},{5,13},{6,14},{7,15},{16,24},{17,25},{..., dimensions={0}, use_global_device_ids=true | all-gather | bytes 49152 | tf_op jit(solution)/shard_map/all_gather | solution.py:514
  31.1 0.0 copy-done
  31.1 0.0 copy-done.1
  31.1 0.0 copy-done.2
  31.1 0.0 copy-done.3
  31.1 3.0 %vessel.1 = (f32[128,128]{1,0:T(8,128)}, f32[128,128]{1,0:T(8,128)}) custom-call(f32[576,128]{1,0:T(8,128)S(1)} %get-tuple-element.6.chip_ref, f32[576,128]{1,0:T(8,128)S(1)} %all_gather.18.slabs_ref, f32[64,128]{1,0:T(8,128)S(1)} %all_gather.19.rows_ref, s32[128,128]{1,0:T(8,128)S(1)} %bitcast.9, bf16[3,384,256]{2,1,0:T(8,128)(2,1)S(1)} %copy-done.1, ...), custom_call_target="tpu_custom_call" | custom-call | tf_op jit(solution)/shard_map/vessel/pallas_call | solution.py:591
  (2 shorter events, 0.0 us)
Async XLA Ops:
  6.2 24.9 %copy-start = (bf16[9,256,256]{2,1,0:T(8,128)(2,1)S(1)}, bf16[9,256,256]{2,1,0:T(8,128)(2,1)}, u32[]{:S(2)}) copy-start(bf16[9,256,256]{2,1,0:T(8,128)(2,1)} %constant.24.clone.y_ref) | copy-start | bytes 3538948
  6.2 24.9 %copy-start.1 = (bf16[3,384,256]{2,1,0:T(8,128)(2,1)S(1)}, bf16[3,384,256]{2,1,0:T(8,128)(2,1)}, u32[]{:S(2)}) copy-start(bf16[3,384,256]{2,1,0:T(8,128)(2,1)} %constant.22.clone.x_upper_ref) | copy-start | bytes 1769476
  6.2 24.8 %copy-start.2 = (bf16[3,384,256]{2,1,0:T(8,128)(2,1)S(1)}, bf16[3,384,256]{2,1,0:T(8,128)(2,1)}, u32[]{:S(2)}) copy-start(bf16[3,384,256]{2,1,0:T(8,128)(2,1)} %constant.23.clone.x_lower_ref) | copy-start | bytes 1769476
  6.2 24.8 %copy-start.3 = (s32[8,16,128]{2,1,0:T(8,128)S(1)}, s32[8,16,128]{2,1,0:T(8,128)}, u32[]{:S(2)}) copy-start(s32[8,16,128]{2,1,0:T(8,128)} %param.16) | copy-start | bytes 196612

commit v4 on v3

--- a/solution.py
+++ b/solution.py
@@ -16,7 +16,9 @@
 SPAN_X = CX + 2 * MARGIN
 HALF = SPAN_X // 2
 ROWS = SPAN_Z * CHANNELS
-SLOT = 512
+SLOT = ROWS + 3 * CHANNELS
+REACH = 5 * CHANNELS
+BLOCKS = ((0, 3), (3, 3), (6, 2), (8, 2))
 RADII = (RIM // 4, RIM // 2, RIM)
 VESSEL_GAIN = 4.0
 TUBE_FLOOR = 0.01
@@ -64,66 +66,55 @@
 
 
 def filter_constants():
-    x_upper, x_lower, y_all = [], [], []
+    x_all, y_all = [], []
     for radius in RADII:
-        blocks = [
-            np.kron(np.eye(CZ), band(CX, CX + 2 * RIM, RIM, radius, degree)) for degree in range(3)
-        ]
+        blocks = [band(CX, CX + 2 * RIM, RIM, radius, degree) for degree in range(3)]
         upper, lower = split_terms(np.concatenate(blocks, axis=0))
-        x_upper.append(upper)
-        x_lower.append(lower)
+        x_all.append(np.concatenate([upper, upper, lower], axis=1))
         for degree in range(3):
             scaled = (radius / 3.0) ** 2 * band(YC, YC, 0, radius, degree).T
             upper, lower = split_terms(scaled)
             top = np.concatenate([upper, lower], axis=1)
             bottom = np.concatenate([upper, np.zeros_like(lower)], axis=1)
             y_all.append(np.concatenate([top, bottom], axis=0))
-    return np.stack(x_upper), np.stack(x_lower), np.stack(y_all)
+    return np.stack(x_all), np.stack(y_all)
 
 
 def iota(shape, dim):
     return lax.broadcasted_iota(jnp.int32, shape, dim)
 
 
-def y_neighbours(values):
-    lane = iota(values.shape, 1)
-    before = jnp.where(lane == 0, 0.0, pltpu.roll(values, 1, 1))
-    after = jnp.where(lane == YC - 1, 0.0, pltpu.roll(values, YC - 1, 1))
-    return (before, values, after)
-
-
-def store_column(slots_ref, slot, half, three):
-    lanes = pl.ds(half * YC, YC)
-    for dy in range(3):
-        slots_ref[pl.ds(slot * SLOT + dy * ROWS, ROWS), lanes] = three[dy]
+def sum_over_y(parts):
+    lane = iota(parts[0].shape, 1)
+    before = jnp.where(lane == 0, 0.0, pltpu.roll(parts[0], 1, 1))
+    after = jnp.where(lane == YC - 1, 0.0, pltpu.roll(parts[2], YC - 1, 1))
+    return before + parts[1] + after
+
+
+def store_part(slots_ref, slot, half, z, part):
+    at = slot * SLOT + (z + 1) * CHANNELS
+    slots_ref[at : at + part.shape[0], half * YC : (half + 1) * YC] = part
 
 
 def expand_weight(weight_ref, wide_ref):
-    lane = iota((CHANNELS, SLOT), 1)
-    group = (lane >= ROWS).astype(jnp.int32) + (lane >= 2 * ROWS).astype(jnp.int32) + (
-        lane >= 3 * ROWS
-    ).astype(jnp.int32)
-    row = iota((CHANNELS, SLOT), 0)
-    same = (lane & (CHANNELS - 1)) == row
-    spread = jnp.zeros((9 * CHANNELS, SLOT), jnp.float32)
-    for dy in range(3):
-        pick = jnp.where(same & (group == dy), 1.0, 0.0).astype(jnp.bfloat16)
-        part = weight_ref[:, :, dy].reshape(9 * CHANNELS, CHANNELS)
+    shape = (CHANNELS, 3 * REACH)
+    lane = iota(shape, 1)
+    group = (lane >= REACH).astype(jnp.int32) + (lane >= 2 * REACH).astype(jnp.int32)
+    same = (lane & (CHANNELS - 1)) == iota(shape, 0)
+    spread = jnp.zeros((9 * CHANNELS, 3 * REACH), jnp.float32)
+    for dx in range(3):
+        pick = jnp.where(same & (group == dx), 1.0, 0.0).astype(jnp.bfloat16)
+        part = weight_ref[:, dx].reshape(9 * CHANNELS, CHANNELS)
         spread = spread + jnp.dot(part, pick, preferred_element_type=jnp.float32)
-    plane = (lane - group * ROWS) >> 4
-    for dx in range(3):
-        three = [
-            spread[(dz * 3 + dx) * CHANNELS : (dz * 3 + dx + 1) * CHANNELS] for dz in range(3)
-        ]
-        for z in range(SPAN_Z):
-            rows = jnp.where(
-                plane == z - 1,
-                three[0],
-                jnp.where(plane == z, three[1], jnp.where(plane == z + 1, three[2], 0.0)),
-            )
-            wide_ref[z * CHANNELS : (z + 1) * CHANNELS, dx * SLOT : (dx + 1) * SLOT] = rows.astype(
-                jnp.bfloat16
-            )
+    plane = (lane - group * REACH) >> 4
+    for z in range(3):
+        for dy in range(3):
+            rows = jnp.zeros(shape, jnp.float32)
+            for dz in range(3):
+                at = (dz * 3 + dy) * CHANNELS
+                rows = jnp.where(plane == z + dz, spread[at : at + CHANNELS], rows)
+            at = (z * 3 + dy) * CHANNELS
+            wide_ref[at : at + CHANNELS, :] = rows.astype(jnp.bfloat16)
 
 
 def column_of(row_ref):
@@ -171,8 +162,10 @@
         ref[0:SLOT, 0:YC] = jnp.zeros((SLOT, YC), jnp.bfloat16)
         ref[(HALF + 1) * SLOT :, YC:] = jnp.zeros((SLOT, YC), jnp.bfloat16)
         for slot in range(HALF + 2):
-            ref[slot * SLOT + 3 * ROWS : (slot + 1) * SLOT, :] = jnp.zeros(
-                (SLOT - 3 * ROWS, 2 * YC), jnp.bfloat16
+            base = slot * SLOT
+            ref[base : base + CHANNELS, :] = jnp.zeros((CHANNELS, 2 * YC), jnp.bfloat16)
+            ref[base + CHANNELS + ROWS : base + SLOT, :] = jnp.zeros(
+                (2 * CHANNELS, 2 * YC), jnp.bfloat16
             )
     copies[0].wait()
     expand_weight(weight1_ref, wide1_ref)
@@ -181,33 +174,43 @@
     for copy in copies[2:]:
         copy.wait()
     for x in range(SPAN_X):
-        column = features_ref[:, x].reshape(ROWS, YC).astype(jnp.float32)
-        three = [v.astype(jnp.bfloat16) for v in y_neighbours(column)]
+        column = features_ref[:, x].reshape(ROWS, YC)
         if x <= HALF:
-            store_column(first_ref, x + 1, 0, three)
+            store_part(first_ref, x + 1, 0, 0, column)
         if x >= HALF - 1:
-            store_column(first_ref, x - HALF + 1, 1, three)
-
-    def layer(wide_ref, slots_ref, bias, step):
-        summed = jnp.dot(
-            wide_ref[...],
-            slots_ref[step * SLOT : (step + 3) * SLOT, :],
-            preferred_element_type=jnp.float32,
-        )
-        shaped = summed.reshape(SPAN_Z, CHANNELS, 2 * YC) + bias[None]
-        return jnp.maximum(shaped, 0.0).reshape(ROWS, 2 * YC)
+            store_part(first_ref, x - HALF + 1, 1, 0, column)
+
+    def layer(wide_ref, slots_ref, bias, step, put):
+        for first, count in BLOCKS:
+            pieces = []
+            for dx in range(3):
+                at = (step + dx) * SLOT + first * CHANNELS
+                pieces.append(slots_ref[at : at + REACH, :])
+            summed = jnp.dot(
+                wide_ref[: count * 3 * CHANNELS],
+                jnp.concatenate(pieces, axis=0),
+                preferred_element_type=jnp.float32,
+            )
+            for z in range(count):
+                for half in range(2):
+                    parts = []
+                    for dy in range(3):
+                        at = (z * 3 + dy) * CHANNELS
+                        parts.append(summed[at : at + CHANNELS, half * YC : (half + 1) * YC])
+                    value = jnp.maximum(sum_over_y(parts) + bias, 0.0)
+                    put(first + z, half, value.astype(jnp.bfloat16))
 
     bias1 = column_of(bias1_ref)
     for step in range(HALF):
-        hidden = layer(wide1_ref, first_ref, bias1, step)
-        for half in range(2):
-            part = hidden[:, half * YC : (half + 1) * YC]
-            three = [v.astype(jnp.bfloat16) for v in y_neighbours(part)]
-            store_column(second_ref, step + 1, half, three)
+
+        def put_first(z, half, part, step=step):
+            store_part(second_ref, step + 1, half, z, part)
             if half == 0 and step == HALF - 1:
-                store_column(second_ref, 0, 1, three)
+                store_part(second_ref, 0, 1, z, part)
             if half == 1 and step == 0:
-                store_column(second_ref, HALF + 1, 0, three)
+                store_part(second_ref, HALF + 1, 0, z, part)
+
+        layer(wide1_ref, first_ref, bias1, step, put_first)
 
     bias2 = column_of(bias2_ref)
     repeat = ((iota((CHANNELS, ROWS), 1) & (CHANNELS - 1)) == iota((CHANNELS, ROWS), 0)).astype(
@@ -223,8 +226,12 @@
     centred = (place - (SPAN_Z - 1) / 2.0) / (SPAN_Z / 4.0)
     weight_z = jnp.exp(-0.5 * centred * centred)
     for step in range(HALF):
-        hidden = layer(wide2_ref, second_ref, bias2, step).astype(jnp.bfloat16)
-        last_ref[:, step * 2 * YC : (step + 1) * 2 * YC] = hidden
+
+        def put_last(z, half, part, step=step):
+            at = (step * 2 + half) * YC
+            last_ref[z * CHANNELS : (z + 1) * CHANNELS, at : at + YC] = part
+
+        layer(wide2_ref, second_ref, bias2, step, put_last)
     logits = jnp.dot(head, last_ref[...], preferred_element_type=jnp.float32)
     for step in range(HALF):
         for half in range(2):
@@ -331,8 +338,7 @@
     slabs_ref,
     rows_ref,
     tissue_ref,
-    x_upper_ref,
-    x_lower_ref,
+    x_ref,
     y_ref,
     probability_ref,
     vessel_ref,
@@ -416,50 +422,44 @@
 
     weights = [[taps(radius, degree) for degree in range(3)] for radius in RADII]
 
-    def one_plane(i, carry):
-        def plane(offset):
-            return extended_ref[pl.ds(pl.multiple_of((i + RIM + offset) * 32, 32), 32), :]
-
-        centre = plane(0)
-        results = {}
-        for n, radius in enumerate(RADII):
-            for degree in (0, 2):
-                results[n, degree] = centre * float(weights[n][degree][radius])
-        for k in range(1, RIM + 1):
-            before, after = plane(-k), plane(k)
-            both, change = before + after, before - after
-            for n, radius in enumerate(RADII):
-                if k > radius:
-                    continue
+    def filter_z(n, radius):
+        for i in range(CZ):
+
+            def plane(offset):
+                at = (i + RIM + offset) * 32
+                return extended_ref[at : at + 32, :]
+
+            centre = plane(0)
+            results = [centre * float(weights[n][degree][radius]) for degree in range(3)]
+            for k in range(1, radius + 1):
+                before, after = plane(-k), plane(k)
+                both, change = before + after, before - after
                 for degree in range(3):
                     term = (change if degree == 1 else both) * float(weights[n][degree][radius + k])
-                    if (n, degree) in results:
-                        results[n, degree] = results[n, degree] + term
-                    else:
-                        results[n, degree] = term
-        for n in range(3):
+                    fresh = degree == 1 and k == 1
+                    results[degree] = term if fresh else results[degree] + term
             for degree in range(3):
-                upper, lower = two_terms(results[n, degree])
-                rows = pl.ds(pl.multiple_of((n * 3 + degree) * 256 + i * 32, 32), 32)
-                along_z_ref[rows, 0:YC] = upper
-                along_z_ref[rows, YC : 2 * YC] = lower
-        return carry
-
-    lax.fori_loop(0, CZ, one_plane, 0)
+                upper, lower = two_terms(results[degree])
+                base = (n * 3 + degree) * 96
+                for at, part in ((0, upper), (32, lower), (64, upper)):
+                    along_z_ref[base + at : base + at + 32, i * YC : (i + 1) * YC] = part
 
     total = jnp.zeros((CZ * CX, YC), jnp.float32)
+    filter_z(0, RADII[0])
     for n in range(3):
+        if n < 2:
+            filter_z(n + 1, RADII[n + 1])
         after_x = {}
         for degree in range(3):
-            count = (3 - degree) * 128
-            data = along_z_ref[(n * 3 + degree) * 256 : (n * 3 + degree + 1) * 256, :]
-            wide = jnp.dot(x_upper_ref[n, :count], data, preferred_element_type=jnp.float32)
-            narrow = jnp.dot(
-                x_lower_ref[n, :count], data[:, :YC], preferred_element_type=jnp.float32
+            data = along_z_ref[(n * 3 + degree) * 96 : (n * 3 + degree + 1) * 96, :]
+            wide = jnp.dot(
+                x_ref[n, : (3 - degree) * CX], data, preferred_element_type=jnp.float32
             )
-            summed = wide[:, :YC] + wide[:, YC:] + narrow
             for other in range(3 - degree):
-                after_x[degree, other] = summed[other * 128 : (other + 1) * 128]
+                rows = wide[other * CX : (other + 1) * CX]
+                after_x[degree, other] = jnp.concatenate(
+                    [rows[:, z * YC : (z + 1) * YC] for z in range(CZ)], axis=0
+                )
 
         def along_y(degree, keys):
             stacked = jnp.concatenate([after_x[key] for key in keys], axis=0)
@@ -540,8 +540,8 @@
             pltpu.VMEM((1, CHANNELS), bf16),
             pltpu.VMEM(slots, bf16),
             pltpu.VMEM(slots, bf16),
-            pltpu.VMEM((ROWS, 3 * SLOT), bf16),
-            pltpu.VMEM((ROWS, 3 * SLOT), bf16),
+            pltpu.VMEM((9 * CHANNELS, 3 * REACH), bf16),
+            pltpu.VMEM((9 * CHANNELS, 3 * REACH), bf16),
             pltpu.VMEM((ROWS, SPAN_X * YC), bf16),
             pltpu.SemaphoreType.DMA((6,)),
         ],
@@ -557,10 +557,34 @@
     )
 
 
+def measure_tubes(chip, slabs, rows, tissue_mask):
+    f32, bf16 = jnp.float32, jnp.bfloat16
+    params = pltpu.CompilerParams(vmem_limit_bytes=VMEM_LIMIT)
+    x_all, y_all = filter_constants()
+    return pl.pallas_call(
+        vessel_kernel,
+        out_shape=(shape_of(CZ * CX, YC), shape_of(CZ * CX, YC)),
+        in_specs=whole(6),
+        out_specs=tuple(whole(2)),
+        scratch_shapes=[
+            pltpu.VMEM((3 * CZ * 32, YC), f32),
+            pltpu.VMEM((9 * 96, CZ * YC), bf16),
+        ],
+        compiler_params=params,
+        name="vessel",
+    )(
+        chip,
+        slabs,
+        rows,
+        tissue_mask.reshape(CZ * CX, YC),
+        jnp.asarray(x_all),
+        jnp.asarray(y_all),
+    )
+
+
 def on_device(
     patch_features, conv1_weight, conv1_bias, conv2_weight, conv2_bias, head_weight, tissue_mask
 ):
-    f32, bf16 = jnp.float32, jnp.bfloat16
     params = pltpu.CompilerParams(vmem_limit_bytes=VMEM_LIMIT)
     patch = decode(
         patch_features, conv1_weight, conv1_bias, conv2_weight, conv2_bias, head_weight
@@ -587,27 +611,7 @@
     upper_core = lax.axis_index("gz") & 1
     row_at = jnp.where(upper_core == 1, SEND_ROWS * 32, (SEND_ROWS - 1) * 32)
     rows = swap(lax.dynamic_slice(slabs, (row_at, 0), (32, YC)), "chip")
-    x_upper, x_lower, y_all = filter_constants()
-    probability, vesselness = pl.pallas_call(
-        vessel_kernel,
-        out_shape=(shape_of(CZ * CX, YC), shape_of(CZ * CX, YC)),
-        in_specs=whole(7),
-        out_specs=tuple(whole(2)),
-        scratch_shapes=[
-            pltpu.VMEM((3 * CZ * 32, YC), f32),
-            pltpu.VMEM((9 * 256, 2 * YC), bf16),
-        ],
-        compiler_params=params,
-        name="vessel",
-    )(
-        chip,
-        slabs,
-        rows,
-        tissue_mask.reshape(CZ * CX, YC),
-        jnp.asarray(x_upper),
-        jnp.asarray(x_lower),
-        jnp.asarray(y_all),
-    )
+    probability, vesselness = measure_tubes(chip, slabs, rows, tissue_mask)
     return (
         probability.reshape(CZ, CX, YC),
         vesselness.reshape(CZ, CX, YC),

time: 34.2 us -> 32.5 us (0.950)
  Pallas kernels: 8.77 us -> 7.06 us
    pallas_call x1, Pallas kernels: 5.56 us -> 4.32 us  [decode(): pl.pallas_call(decoder_kernel, out_shape=shape_of(PATCH, YC), in_specs=wh...]
    pallas_call x1, Pallas kernels: 2.99 us -> 2.5 us  [measure_tubes(): pl.pallas_call(vessel_kernel, out_shape=(shape_of(CZ * CX, YC), shape_of(...]
where the time goes in v4:
time: 32.5 us; the launch traced here: 32.3 us
  blocking collectives  24.6 us (76%)
  Pallas kernels  7.06 us (22%)
  between operations  0.68 us (2%)
    all_gather x5, blocking collectives, swap(): lax.all_gather(block, ('gz', 'xy'), axis_index_groups=groups, tiled=True)  24.6 us
    pallas_call x1, Pallas kernels, decode(): pl.pallas_call(decoder_kernel, out_shape=shape_of(PATCH, YC), in_specs=wh...  4.32 us
    pallas_call x1, Pallas kernels, measure_tubes(): pl.pallas_call(vessel_kernel, out_shape=(shape_of(CZ * CX, YC), shape_of(...  2.5 us

profile of v4, /device:TPU:1, one launch (start us, length us, event | category | flops | bytes accessed | tf_op | source)
XLA Modules:
  0.0 32.3 jit_solution(14622461572410619793)
XLA Ops:
  0.6 4.3 %decoder.1 = f32[192,128]{1,0:T(8,128)} custom-call(bf16[10,18,16,128]{3,2,1,0:T(8,128)(2,1)} %bitcast.10, bf16[3,3,3,16,16]{4,3,2,1,0:T(8,128)(2,1)} %bitcast.11, f32[1,16]{1,0:T(1,128)} %bitcast.13, bf16[3,3,3,16,16]{4,3,2,1,0:T(8,128)(2,1)} %bitcast.12, f32[1,16]{1,0:T(1,128)} %bitcast.14, bf16[1,16]{1,0:T(2,128)(2,1)} %bitcast.15), custom_call_target="tpu_custom_call" | custom-call | tf_op jit(solution)/shard_map/decoder/pallas_call | solution.py:529
  5.0 0.0 copy-start
  5.0 0.0 copy-start.1
  5.0 0.0 copy-start.2
  5.0 8.8 %all_gather.15.pair_ref = f32[384,128]{1,0:T(8,128)S(1)} all-gather(f32[192,128]{1,0:T(8,128)} %decoder.1), channel_id=1, replica_groups={{0,8},{1,9},{2,10},{3,11},{4,12},{5,13},{6,14},{7,15},{16,24},{17,25},{..., dimensions={0}, use_global_device_ids=true | all-gather | bytes 294912 | tf_op jit(solution)/shard_map/all_gather | solution.py:514
  13.8 4.3 %all_gather.16 = f32[336,128]{1,0:T(8,128)S(1)} all-gather(f32[168,128]{1,0:T(8,128)S(1)} %edge.1), channel_id=1, replica_groups={{0,1},{2,3},{4,5},{6,7},{9,10},{11,12},{13,14},{16,17},{18,19},{20,21},..., dimensions={0}, use_global_device_ids=true | all-gather | bytes 258048 | tf_op jit(solution)/shard_map/all_gather | solution.py:514
  18.2 2.9 %all_gather.17.edges_ref = f32[672,128]{1,0:T(8,128)S(1)} all-gather(f32[336,128]{1,0:T(8,128)S(1)} %all_gather.16), channel_id=1, replica_groups={{0,8},{1,9},{2,10},{3,11},{4,12},{5,13},{6,14},{7,15},{16,24},{17,25},{..., dimensions={0}, use_global_device_ids=true | all-gather | bytes 516096 | tf_op jit(solution)/shard_map/all_gather | solution.py:514
  21.0 0.2 chip.1
  21.2 6.7 %all_gather.18.slabs_ref = f32[576,128]{1,0:T(8,128)S(1)} all-gather(f32[288,128]{1,0:T(8,128)S(1)} %get-tuple-element.7), channel_id=1, replica_groups={{8,16},{9,17},{10,18},{11,19},{12,20},{13,21},{14,22},{15,23},{24,32},{..., dimensions={0}, use_global_device_ids=true | all-gather | bytes 442368 | tf_op jit(solution)/shard_map/all_gather | solution.py:514
  28.0 1.8 %all_gather.19.rows_ref = f32[64,128]{1,0:T(8,128)S(1)} all-gather(f32[32,128]{1,0:T(8,128)S(1)} %constant_dynamic-slice_fusion), channel_id=1, replica_groups={{0,8},{1,9},{2,10},{3,11},{4,12},{5,13},{6,14},{7,15},{16,24},{17,25},{..., dimensions={0}, use_global_device_ids=true | all-gather | bytes 49152 | tf_op jit(solution)/shard_map/all_gather | solution.py:514
  29.8 0.0 copy-done
  29.8 0.0 copy-done.1
  29.8 0.0 copy-done.2
  29.8 2.5 %vessel.1 = (f32[128,128]{1,0:T(8,128)}, f32[128,128]{1,0:T(8,128)}) custom-call(f32[576,128]{1,0:T(8,128)S(1)} %get-tuple-element.6.chip_ref, f32[576,128]{1,0:T(8,128)S(1)} %all_gather.18.slabs_ref, f32[64,128]{1,0:T(8,128)S(1)} %all_gather.19.rows_ref, s32[128,128]{1,0:T(8,128)S(1)} %bitcast.9, bf16[3,48,96]{2,1,0:T(8,128)(2,1)S(1)} %copy-done.2, ...), custom_call_target="tpu_custom_call" | custom-call | tf_op jit(solution)/shard_map/vessel/pallas_call | solution.py:564
  (2 shorter events, 0.0 us)
Async XLA Ops:
  5.0 24.9 %copy-start = (bf16[9,256,256]{2,1,0:T(8,128)(2,1)S(1)}, bf16[9,256,256]{2,1,0:T(8,128)(2,1)}, u32[]{:S(2)}) copy-start(bf16[9,256,256]{2,1,0:T(8,128)(2,1)} %constant.21.clone.y_ref) | copy-start | bytes 3538948
  5.0 24.8 %copy-start.1 = (s32[8,16,128]{2,1,0:T(8,128)S(1)}, s32[8,16,128]{2,1,0:T(8,128)}, u32[]{:S(2)}) copy-start(s32[8,16,128]{2,1,0:T(8,128)} %param.15) | copy-start | bytes 196612
  5.0 24.8 %copy-start.2 = (bf16[3,48,96]{2,1,0:T(8,128)(2,1)S(1)}, bf16[3,48,96]{2,1,0:T(8,128)(2,1)}, u32[]{:S(2)}) copy-start(bf16[3,48,96]{2,1,0:T(8,128)(2,1)} %constant.20.clone.x_ref) | copy-start | bytes 82948

commit v5 on v4

--- a/solution.py
+++ b/solution.py
@@ -361,7 +361,7 @@
                 part = slabs_ref[z * 32 : (z + 1) * 32, :] * below
                 value = part if value is None else value + part
             if z == 3 * CZ - 1:
-                value = value + rows_ref[32:64, :] * above
+                value = value + rows_ref[96:128, :] * above
             extended_ref[z * 32 : (z + 1) * 32, :] = value
 
     @pl.when(upper_core)
@@ -608,9 +608,8 @@
         name="chip",
     )(pair, edges)
     slabs = swap(send, "slab")
-    upper_core = lax.axis_index("gz") & 1
-    row_at = jnp.where(upper_core == 1, SEND_ROWS * 32, (SEND_ROWS - 1) * 32)
-    rows = swap(lax.dynamic_slice(slabs, (row_at, 0), (32, YC)), "chip")
+    near = (SEND_ROWS - 1) * 32
+    rows = swap(slabs[near : near + 64], "chip")
     probability, vesselness = measure_tubes(chip, slabs, rows, tissue_mask)
     return (
         probability.reshape(CZ, CX, YC),

time: 32.5 us -> 32.5 us (level)
  no operation moved by 1% of the time
where the time goes in v5:
time: 32.5 us; the launch traced here: 32.4 us
  blocking collectives  24.6 us (76%)
  Pallas kernels  7.06 us (22%)
  between operations  0.68 us (2%)
    all_gather x5, blocking collectives, swap(): lax.all_gather(block, ('gz', 'xy'), axis_index_groups=groups, tiled=True)  24.6 us
    pallas_call x1, Pallas kernels, decode(): pl.pallas_call(decoder_kernel, out_shape=shape_of(PATCH, YC), in_specs=wh...  4.32 us
    pallas_call x1, Pallas kernels, measure_tubes(): pl.pallas_call(vessel_kernel, out_shape=(shape_of(CZ * CX, YC), shape_of(...  2.5 us

profile of v5, /device:TPU:1, one launch (start us, length us, event | category | flops | bytes accessed | tf_op | source)
XLA Modules:
  0.0 32.4 jit_solution(9359707295027579551)
XLA Ops:
  0.6 4.3 %decoder.1 = f32[192,128]{1,0:T(8,128)} custom-call(bf16[10,18,16,128]{3,2,1,0:T(8,128)(2,1)} %bitcast.10, bf16[3,3,3,16,16]{4,3,2,1,0:T(8,128)(2,1)} %bitcast.11, f32[1,16]{1,0:T(1,128)} %bitcast.13, bf16[3,3,3,16,16]{4,3,2,1,0:T(8,128)(2,1)} %bitcast.12, f32[1,16]{1,0:T(1,128)} %bitcast.14, bf16[1,16]{1,0:T(2,128)(2,1)} %bitcast.15), custom_call_target="tpu_custom_call" | custom-call | tf_op jit(solution)/shard_map/decoder/pallas_call | solution.py:529
  5.0 0.0 copy-start
  5.0 0.0 copy-start.1
  5.0 0.0 copy-start.2
  5.0 8.8 %all_gather.15.pair_ref = f32[384,128]{1,0:T(8,128)S(1)} all-gather(f32[192,128]{1,0:T(8,128)} %decoder.1), channel_id=1, replica_groups={{0,8},{1,9},{2,10},{3,11},{4,12},{5,13},{6,14},{7,15},{16,24},{17,25},{..., dimensions={0}, use_global_device_ids=true | all-gather | bytes 294912 | tf_op jit(solution)/shard_map/all_gather | solution.py:514
  13.8 4.3 %all_gather.16 = f32[336,128]{1,0:T(8,128)S(1)} all-gather(f32[168,128]{1,0:T(8,128)S(1)} %edge.1), channel_id=1, replica_groups={{0,1},{2,3},{4,5},{6,7},{9,10},{11,12},{13,14},{16,17},{18,19},{20,21},..., dimensions={0}, use_global_device_ids=true | all-gather | bytes 258048 | tf_op jit(solution)/shard_map/all_gather | solution.py:514
  18.2 2.9 %all_gather.17.edges_ref = f32[672,128]{1,0:T(8,128)S(1)} all-gather(f32[336,128]{1,0:T(8,128)S(1)} %all_gather.16), channel_id=1, replica_groups={{0,8},{1,9},{2,10},{3,11},{4,12},{5,13},{6,14},{7,15},{16,24},{17,25},{..., dimensions={0}, use_global_device_ids=true | all-gather | bytes 516096 | tf_op jit(solution)/shard_map/all_gather | solution.py:514
  21.0 0.2 chip.1
  21.2 6.7 %all_gather.18.slabs_ref = f32[576,128]{1,0:T(8,128)S(1)} all-gather(f32[288,128]{1,0:T(8,128)S(1)} %get-tuple-element.7), channel_id=1, replica_groups={{8,16},{9,17},{10,18},{11,19},{12,20},{13,21},{14,22},{15,23},{24,32},{..., dimensions={0}, use_global_device_ids=true | all-gather | bytes 442368 | tf_op jit(solution)/shard_map/all_gather | solution.py:514
  28.0 1.8 %all_gather.19.rows_ref = f32[128,128]{1,0:T(8,128)S(1)} all-gather(f32[64,128]{1,0:T(8,128)S(1)} %slice.4), channel_id=1, replica_groups={{0,8},{1,9},{2,10},{3,11},{4,12},{5,13},{6,14},{7,15},{16,24},{17,25},{..., dimensions={0}, use_global_device_ids=true | all-gather | bytes 98304 | tf_op jit(solution)/shard_map/all_gather | solution.py:514
  29.8 0.0 copy-done
  29.8 0.0 copy-done.1
  29.8 0.0 copy-done.2
  29.9 2.5 %vessel.1 = (f32[128,128]{1,0:T(8,128)}, f32[128,128]{1,0:T(8,128)}) custom-call(f32[576,128]{1,0:T(8,128)S(1)} %get-tuple-element.6.chip_ref, f32[576,128]{1,0:T(8,128)S(1)} %all_gather.18.slabs_ref, f32[128,128]{1,0:T(8,128)S(1)} %all_gather.19.rows_ref, s32[128,128]{1,0:T(8,128)S(1)} %bitcast.9, bf16[3,48,96]{2,1,0:T(8,128)(2,1)S(1)} %copy-done.2, ...), custom_call_target="tpu_custom_call" | custom-call | tf_op jit(solution)/shard_map/vessel/pallas_call | solution.py:564
  (2 shorter events, 0.0 us)
Async XLA Ops:
  5.0 24.9 %copy-start = (bf16[9,256,256]{2,1,0:T(8,128)(2,1)S(1)}, bf16[9,256,256]{2,1,0:T(8,128)(2,1)}, u32[]{:S(2)}) copy-start(bf16[9,256,256]{2,1,0:T(8,128)(2,1)} %constant.5.clone.y_ref) | copy-start | bytes 3538948
  5.0 24.9 %copy-start.1 = (s32[8,16,128]{2,1,0:T(8,128)S(1)}, s32[8,16,128]{2,1,0:T(8,128)}, u32[]{:S(2)}) copy-start(s32[8,16,128]{2,1,0:T(8,128)} %param.15) | copy-start | bytes 196612
  5.0 24.9 %copy-start.2 = (bf16[3,48,96]{2,1,0:T(8,128)(2,1)S(1)}, bf16[3,48,96]{2,1,0:T(8,128)(2,1)}, u32[]{:S(2)}) copy-start(bf16[3,48,96]{2,1,0:T(8,128)(2,1)} %constant.4.clone.x_ref) | copy-start | bytes 82948

commit v6 on v4

--- a/solution.py
+++ b/solution.py
@@ -141,7 +141,6 @@
     second_ref,
     wide1_ref,
     wide2_ref,
-    last_ref,
     arrived,
 ):
     routes = (
@@ -213,36 +212,23 @@
         layer(wide1_ref, first_ref, bias1, step, put_first)
 
     bias2 = column_of(bias2_ref)
-    repeat = ((iota((CHANNELS, ROWS), 1) & (CHANNELS - 1)) == iota((CHANNELS, ROWS), 0)).astype(
-        jnp.float32
-    )
-    head_lanes = jnp.sum(
-        repeat * column_of(head_ref), axis=0, keepdims=True
-    )
-    head = jnp.where(
-        (iota((16, ROWS), 1) >> 4) == iota((16, ROWS), 0), head_lanes, 0.0
-    ).astype(jnp.bfloat16)
-    place = iota((16, YC), 0).astype(jnp.float32)
-    centred = (place - (SPAN_Z - 1) / 2.0) / (SPAN_Z / 4.0)
-    weight_z = jnp.exp(-0.5 * centred * centred)
+    head_column = column_of(head_ref)
+    patch_ref[SPAN_Z * CX :, :] = jnp.zeros((PATCH - SPAN_Z * CX, YC), jnp.float32)
     for step in range(HALF):
 
         def put_last(z, half, part, step=step):
-            at = (step * 2 + half) * YC
-            last_ref[z * CHANNELS : (z + 1) * CHANNELS, at : at + YC] = part
+            x = step + half * HALF
+            scaled = part.astype(jnp.float32) * head_column
+            logit = jnp.sum(scaled, axis=0, keepdims=True)
+            weighted = logit * float(WINDOW_Z[z] * WINDOW_X[x])
+            at = z * CX + x - 1
+            if x == 0:
+                at = SPAN_Z * CX + z
+            elif x == SPAN_X - 1:
+                at = SPAN_Z * CX + 16 + z
+            patch_ref[at : at + 1, :] = weighted
 
         layer(wide2_ref, second_ref, bias2, step, put_last)
-    logits = jnp.dot(head, last_ref[...], preferred_element_type=jnp.float32)
-    for step in range(HALF):
-        for half in range(2):
-            x = step + half * HALF
-            at = (step * 2 + half) * YC
-            weighted = logits[:, at : at + YC] * (weight_z * float(WINDOW_X[x]))
-            if x == 0 or x == SPAN_X - 1:
-                side = 0 if x == 0 else 1
-                patch_ref[160 + side * 16 : 176 + side * 16, :] = weighted
-            else:
-                patch_ref[pl.ds(x - 1, SPAN_Z, stride=CX), :] = weighted[:SPAN_Z]
 
 
 def chip_row(pair_ref, r):
@@ -542,7 +528,6 @@
             pltpu.VMEM(slots, bf16),
             pltpu.VMEM((9 * CHANNELS, 3 * REACH), bf16),
             pltpu.VMEM((9 * CHANNELS, 3 * REACH), bf16),
-            pltpu.VMEM((ROWS, SPAN_X * YC), bf16),
             pltpu.SemaphoreType.DMA((6,)),
         ],
         compiler_params=pltpu.CompilerParams(vmem_limit_bytes=DECODER_VMEM_LIMIT),

time: 32.5 us -> 32.4 us (level)
  no operation moved by 1% of the time
where the time goes in v6:
time: 32.4 us; the launch traced here: 32.2 us
  blocking collectives  24.6 us (76%)
  Pallas kernels  6.94 us (21%)
  between operations  0.68 us (2%)
    all_gather x5, blocking collectives, swap(): lax.all_gather(block, ('gz', 'xy'), axis_index_groups=groups, tiled=True)  24.6 us
    pallas_call x1, Pallas kernels, decode(): pl.pallas_call(decoder_kernel, out_shape=shape_of(PATCH, YC), in_specs=wh...  4.2 us
    pallas_call x1, Pallas kernels, measure_tubes(): pl.pallas_call(vessel_kernel, out_shape=(shape_of(CZ * CX, YC), shape_of(...  2.5 us

profile of v6, /device:TPU:1, one launch (start us, length us, event | category | flops | bytes accessed | tf_op | source)
XLA Modules:
  0.0 32.2 jit_solution(2833316440622090949)
XLA Ops:
  0.6 4.2 %decoder.1 = f32[192,128]{1,0:T(8,128)} custom-call(bf16[10,18,16,128]{3,2,1,0:T(8,128)(2,1)} %bitcast.10, bf16[3,3,3,16,16]{4,3,2,1,0:T(8,128)(2,1)} %bitcast.11, f32[1,16]{1,0:T(1,128)} %bitcast.13, bf16[3,3,3,16,16]{4,3,2,1,0:T(8,128)(2,1)} %bitcast.12, f32[1,16]{1,0:T(1,128)} %bitcast.14, bf16[1,16]{1,0:T(2,128)(2,1)} %bitcast.15), custom_call_target="tpu_custom_call" | custom-call | tf_op jit(solution)/shard_map/decoder/pallas_call | solution.py:515
  4.8 0.0 copy-start
  4.9 0.0 copy-start.1
  4.9 0.0 copy-start.2
  4.9 8.8 %all_gather.15.pair_ref = f32[384,128]{1,0:T(8,128)S(1)} all-gather(f32[192,128]{1,0:T(8,128)} %decoder.1), channel_id=1, replica_groups={{0,8},{1,9},{2,10},{3,11},{4,12},{5,13},{6,14},{7,15},{16,24},{17,25},{..., dimensions={0}, use_global_device_ids=true | all-gather | bytes 294912 | tf_op jit(solution)/shard_map/all_gather | solution.py:500
  13.7 4.3 %all_gather.16 = f32[336,128]{1,0:T(8,128)S(1)} all-gather(f32[168,128]{1,0:T(8,128)S(1)} %edge.1), channel_id=1, replica_groups={{0,1},{2,3},{4,5},{6,7},{9,10},{11,12},{13,14},{16,17},{18,19},{20,21},..., dimensions={0}, use_global_device_ids=true | all-gather | bytes 258048 | tf_op jit(solution)/shard_map/all_gather | solution.py:500
  18.0 2.9 %all_gather.17.edges_ref = f32[672,128]{1,0:T(8,128)S(1)} all-gather(f32[336,128]{1,0:T(8,128)S(1)} %all_gather.16), channel_id=1, replica_groups={{0,8},{1,9},{2,10},{3,11},{4,12},{5,13},{6,14},{7,15},{16,24},{17,25},{..., dimensions={0}, use_global_device_ids=true | all-gather | bytes 516096 | tf_op jit(solution)/shard_map/all_gather | solution.py:500
  20.9 0.2 chip.1
  21.1 6.7 %all_gather.18.slabs_ref = f32[576,128]{1,0:T(8,128)S(1)} all-gather(f32[288,128]{1,0:T(8,128)S(1)} %get-tuple-element.7), channel_id=1, replica_groups={{8,16},{9,17},{10,18},{11,19},{12,20},{13,21},{14,22},{15,23},{24,32},{..., dimensions={0}, use_global_device_ids=true | all-gather | bytes 442368 | tf_op jit(solution)/shard_map/all_gather | solution.py:500
  27.9 1.8 %all_gather.19.rows_ref = f32[64,128]{1,0:T(8,128)S(1)} all-gather(f32[32,128]{1,0:T(8,128)S(1)} %constant_dynamic-slice_fusion), channel_id=1, replica_groups={{0,8},{1,9},{2,10},{3,11},{4,12},{5,13},{6,14},{7,15},{16,24},{17,25},{..., dimensions={0}, use_global_device_ids=true | all-gather | bytes 49152 | tf_op jit(solution)/shard_map/all_gather | solution.py:500
  29.7 0.0 copy-done
  29.7 0.0 copy-done.1
  29.7 0.0 copy-done.2
  29.7 2.5 %vessel.1 = (f32[128,128]{1,0:T(8,128)}, f32[128,128]{1,0:T(8,128)}) custom-call(f32[576,128]{1,0:T(8,128)S(1)} %get-tuple-element.6.chip_ref, f32[576,128]{1,0:T(8,128)S(1)} %all_gather.18.slabs_ref, f32[64,128]{1,0:T(8,128)S(1)} %all_gather.19.rows_ref, s32[128,128]{1,0:T(8,128)S(1)} %bitcast.9, bf16[3,48,96]{2,1,0:T(8,128)(2,1)S(1)} %copy-done.2, ...), custom_call_target="tpu_custom_call" | custom-call | tf_op jit(solution)/shard_map/vessel/pallas_call | solution.py:549
  (2 shorter events, 0.0 us)
Async XLA Ops:
  4.8 24.9 %copy-start = (bf16[9,256,256]{2,1,0:T(8,128)(2,1)S(1)}, bf16[9,256,256]{2,1,0:T(8,128)(2,1)}, u32[]{:S(2)}) copy-start(bf16[9,256,256]{2,1,0:T(8,128)(2,1)} %constant.21.clone.y_ref) | copy-start | bytes 3538948
  4.9 24.8 %copy-start.1 = (s32[8,16,128]{2,1,0:T(8,128)S(1)}, s32[8,16,128]{2,1,0:T(8,128)}, u32[]{:S(2)}) copy-start(s32[8,16,128]{2,1,0:T(8,128)} %param.15) | copy-start | bytes 196612
  4.9 24.8 %copy-start.2 = (bf16[3,48,96]{2,1,0:T(8,128)(2,1)S(1)}, bf16[3,48,96]{2,1,0:T(8,128)(2,1)}, u32[]{:S(2)}) copy-start(bf16[3,48,96]{2,1,0:T(8,128)(2,1)} %constant.20.clone.x_ref) | copy-start | bytes 82948
